TPU v7x, 32 devices: a whole 2x2x4 slice. The times are simulated.
32 devices in a mesh: dp: 8 (over y, x, core), seq: 4 (over z).
Axes of the slice: x: 2, y: 2, z: 4, core: 2. Of those that a mesh axis runs over, the one named last changes fastest.
Arguments:
- tokens: bfloat16 [24, 1024, 768], P('dp', 'seq'), may hold values from -6 to 6
- cond: bfloat16 [24, 128], P('dp'), may hold values from -6 to 6
- lengths: int32 [24], P('dp'), may hold values from 128 to 1024, as said below
- gain_one: float32 [768], replicated, may hold values from 0.1 to 1.9
- gain_two: float32 [768], replicated, may hold values from 0.1 to 1.9
- w_ada: bfloat16 [128, 4608], replicated, may hold values from -0.5 to 0.5
- b_ada: float32 [4608], replicated, may hold values from -3 to 3
- w_qkv: bfloat16 [768, 2304], replicated, may hold values from -0.21875 to 0.21875
- w_out: bfloat16 [768, 768], replicated, may hold values from -0.3125 to 0.3125
- w_up: bfloat16 [768, 3072], replicated, may hold values from -0.21875 to 0.21875
- b_up: float32 [3072], replicated, may hold values from -3 to 3
- w_down: bfloat16 [3072, 768], replicated, may hold values from -0.109375 to 0.109375
- b_down: float32 [768], replicated, may hold values from -3 to 3
- cotangent: bfloat16 [24, 1024, 768], P('dp', 'seq'), may hold values from -8 to 8
Outputs:
- output: bfloat16 [24, 1024, 768], P('dp', 'seq')
- grad_tokens: float32 [24, 1024, 768], P('dp', 'seq')
- grad_cond: float32 [24, 128], P('dp')
- grad_gain_one: float32 [768], P(('dp', 'seq'))
- grad_gain_two: float32 [768], P(('dp', 'seq'))
- grad_w_ada: float32 [128, 4608], P(None, ('dp', 'seq'))
- grad_b_ada: float32 [4608], P(('dp', 'seq'))
- grad_w_qkv: float32 [768, 2304], P(('dp', 'seq'))
- grad_w_out: float32 [768, 768], P(('dp', 'seq'))
- grad_w_up: float32 [768, 3072], P(('dp', 'seq'))
- grad_b_up: float32 [3072], P(('dp', 'seq'))
- grad_w_down: float32 [3072, 768], P(('dp', 'seq'))
- grad_b_down: float32 [768], P(('dp', 'seq'))
Inputs may be any that keep to these rules, and one draw needn't show every extreme that they name: `lengths`: each length is 128, 512 or 1024, each sequence's drawn independently; some sequence of the batch has 1024 and some other has 128.
All inputs are finite; a program needn't handle non-finite values.
Results may differ from a plain program's by a relative error of at most 0.015.
The roundings to bfloat16 on the way count: a program that leaves them out, or rounds other values in their place, can miss the bound.
Values may be sent and summed in bfloat16 or wider, within the bound.
No kernel may reach another device: no remote copies, remote signals or barrier semaphores. Data moves between devices by JAX's collectives and lax.ppermute only.
A program may use at most 256 MiB of HBM per device.

v0:
```python
import functools

import jax
import jax.numpy as jnp
import numpy as np
from jax import lax
from jax.experimental import pallas as pl
from jax.experimental.pallas import tpu as pltpu
from jax.sharding import PartitionSpec as P

HEADS = 12
HD = 64
EPS = 1e-05
HIGH = lax.Precision.HIGHEST
BF = jnp.bfloat16
F32 = jnp.float32
PACK = 4
BLOCK = PACK * HD
LANES = 128
SPANS = (128, 512, 1024)
SCALE = 1000
GELU_C = float(np.sqrt(2.0 / np.pi))


def nn(left, right):
    return lax.dot_general(left, right, (((1,), (0,)), ((), ())), preferred_element_type=F32)


def nt(left, right):
    return lax.dot_general(left, right, (((1,), (1,)), ((), ())), preferred_element_type=F32)


def normalize(vector):
    average = jnp.mean(vector, axis=-1, keepdims=True)
    centred = vector - average
    inverse = lax.rsqrt(jnp.mean(centred * centred, axis=-1, keepdims=True) + EPS)
    return centred * inverse, inverse


def norm_back(grad_normed, normed, inverse):
    return inverse * (
        grad_normed
        - jnp.mean(grad_normed, axis=-1, keepdims=True)
        - normed * jnp.mean(grad_normed * normed, axis=-1, keepdims=True)
    )


def rows_sum(value):
    return jnp.sum(value, axis=0, keepdims=True)


def head_masks():
    lane = lax.broadcasted_iota(jnp.int32, (1, BLOCK), 1)
    return [(lane // HD == h).astype(F32).astype(BF) for h in range(PACK)]


def swap_halves(value):
    half = HD // 2
    lane = lax.broadcasted_iota(jnp.int32, value.shape, 1)
    ahead = pltpu.roll(value, LANES - half, 1)
    behind = pltpu.roll(value, half, 1)
    return jnp.where(lane % HD < half, ahead, behind)


def arrange_kernel(lengths, tok_ref, cond_ref, *refs):
    parts = tok_ref.shape[0]
    tok_refs, both_ref, order_ref = refs[:parts], refs[parts], refs[parts + 1]
    rank = []
    for s in range(parts):
        ahead = jnp.int32(0)
        for k in range(parts):
            if k < s:
                ahead = ahead + (lengths[k] >= lengths[s]).astype(jnp.int32)
            elif k > s:
                ahead = ahead + (lengths[k] > lengths[s]).astype(jnp.int32)
        rank.append(ahead)
    both_ref[...] = jnp.zeros_like(both_ref)
    for r in range(parts):
        at = jnp.int32(0)
        for k in range(1, parts):
            at = jnp.where(rank[k] == r, k, at)
        tok_refs[r][...] = tok_ref[at]
        width = cond_ref.shape[1]
        both_ref[r : r + 1, :width] = cond_ref[pl.ds(at, 1), :]
        both_ref[r : r + 1, width:] = jnp.full((1, LANES), lengths[at]).astype(F32)
        order_ref[r] = at
        order_ref[parts + r] = rank[r]


def arrange_pulls_kernel(order, pull_ref, *refs):
    for r, ref in enumerate(refs):
        ref[...] = pull_ref[order[r]]


def put_kernel(order, *refs):
    parts = (order.shape[0] - 1)
    step = pl.program_id(0)
    value_ref, moved_ref = refs[:2]
    grads, moves = refs[2 : 2 + parts], refs[2 + parts : 2 + 2 * parts]
    out_ref, grad_ref = refs[2 + 2 * parts :]
    stays = order[parts] == 1
    out_ref[...] = jnp.where(stays, value_ref[...], moved_ref[...])
    for s in range(parts):

        @pl.when((step == s) & stays)
        def _():
            grad_ref[0] = grads[s][...]

        @pl.when((step == s) & ~stays)
        def _():
            grad_ref[0] = moves[s][...].astype(F32)


def prep_kernel(
    place, a_ref, b_ref, c_ref, d_ref, mod_ref, gain_ref, w_ref, cos_ref, sin_ref,
    actt_ref, q_ref, k_ref, v_ref,
):
    step = pl.program_id(0)
    rows, width = a_ref.shape
    source = jnp.where(
        step < 2,
        jnp.where(step == 0, a_ref[...], b_ref[...]),
        jnp.where(step == 2, c_ref[...], d_ref[...]),
    ).astype(F32)
    normed, _ = normalize(source)
    act = (normed * gain_ref[...] * (1.0 + mod_ref[0, 1:2, :]) + mod_ref[0, 0:1, :]).astype(BF)
    actt_ref[...] = act.T
    cosine, sine = cos_ref[...], sin_ref[...]

    def turned(start, out_ref, factor):
        for at in range(0, width, BLOCK):
            both = nn(act, w_ref[:, start + at : start + at + BLOCK])
            for lane in range(0, BLOCK, LANES):
                part = both[:, lane : lane + LANES]
                out_ref[:, at + lane : at + lane + LANES] = (
                    part * cosine + swap_halves(part) * sine
                ).astype(BF) * factor

    @pl.when((place[0] ^ step) * rows < place[1])
    def _():
        turned(width, k_ref, BF(1.0))
        v_ref[...] = nn(act, w_ref[:, 2 * width :]).astype(BF)

    @pl.when(step == 0)
    def _():
        turned(0, q_ref, BF(HD**-0.5))


def attend_kernel(place, q_ref, k_ref, v_ref, mix_ref, lse_ref):
    masks = head_masks()
    lane = lax.broadcasted_iota(jnp.int32, (1, BLOCK), 1)
    narrow = lax.broadcasted_iota(jnp.int32, (1, LANES), 1)

    def work(span):
        queries, keys, values = q_ref[...], k_ref[:span, :], v_ref[:span, :]
        mixed = jnp.zeros(q_ref.shape, F32)
        logs = jnp.zeros((q_ref.shape[0], LANES), F32)
        for head in range(PACK):
            scores = nt(queries * masks[head], keys)
            top = jnp.max(scores, axis=-1, keepdims=True)
            raised = jnp.exp(scores - top)
            total = jnp.sum(raised, axis=-1, keepdims=True)
            probs = (raised * (1.0 / total)).astype(BF)
            mixed = jnp.where(lane // HD == head, nn(probs, values), mixed)
            logs = jnp.where(narrow == head, top + jnp.log(total), logs)
        mix_ref[...] = mixed.astype(BF)
        lse_ref[0] = logs.T[:8, :]

    for span in SPANS:
        pl.when(place[1] == span)(functools.partial(work, span))


def attend_back_kernel(
    more, last, place, q_ref, k_ref, v_ref, g_ref, lse_ref, cosq_ref, sinq_ref, cosk_ref, sink_ref,
    wq_ref, wk_ref, wv_ref, actt_ref, owns_ref, *refs,
):
    refs = list(refs)
    before_ref = refs.pop(0) if more else None
    keep_ref, send_ref = refs.pop(0), refs.pop(0)
    outs = [refs.pop(0) for _ in range(4 if last else 1)]
    share, own_share, grad_q, grad_k, grad_v, weights = refs
    masks = head_masks()
    group = pl.program_id(0)
    rows = q_ref.shape[0]

    def unturn(value, cosine, sine, out_ref):
        for lane in range(0, BLOCK, LANES):
            part = value[:, lane : lane + LANES]
            out_ref[: value.shape[0], lane : lane + LANES] = (
                part * cosine - swap_halves(part) * sine
            ).astype(BF)

    @pl.when(group == 0)
    def _():
        share[...] = jnp.zeros_like(share)
        own_share[...] = jnp.zeros_like(own_share)

    def work(span):
        queries, grads = q_ref[...], g_ref[...]
        query_all = jnp.concatenate([queries * masks[h] for h in range(PACK)], axis=0)
        grad_all = jnp.concatenate([grads * masks[h] for h in range(PACK)], axis=0)
        head = lax.broadcasted_iota(jnp.int32, (BLOCK, 1), 0) // HD
        sides = [(head == h).astype(F32).astype(BF) for h in range(PACK)]
        queries_t, grads_t = queries.T, grads.T
        query_t = jnp.concatenate([queries_t * sides[h] for h in range(PACK)], axis=1)
        grad_t = jnp.concatenate([grads_t * sides[h] for h in range(PACK)], axis=1)
        keys, values = k_ref[:span, :], v_ref[:span, :]
        keys_t = keys.T
        raw_all, pull_all = nn(keys, query_t), nn(values, grad_t)
        turned, probs_all, scores_all = [], [], []
        for h in range(PACK):
            part = slice(h * rows, (h + 1) * rows)
            probs = jnp.exp(raw_all[:, part] - lse_ref[0, h : h + 1, :])
            pull = pull_all[:, part]
            scores = (probs * (pull - rows_sum(probs * pull))).astype(BF)
            probs_all.append(probs.astype(BF))
            scores_all.append(scores)
            turned.append(nn(keys_t[h * HD : (h + 1) * HD], scores))
        grad_v[:span, :] = nn(jnp.concatenate(probs_all, axis=1), grad_all).astype(BF)
        grad_keys = nn(jnp.concatenate(scores_all, axis=1), query_all)
        unturn(grad_keys, cosk_ref[:span, :], sink_ref[:span, :], grad_k)
        grad_queries = jnp.concatenate(turned, axis=0).T * HD**-0.5
        unturn(grad_queries, cosq_ref[...], sinq_ref[...], grad_q)
        share[:span, :] += nt(grad_k[:span, :], wk_ref[...]) + nt(grad_v[:span, :], wv_ref[...])
        act = actt_ref[:, :span]
        products = (
            nn(owns_ref[...], grad_q[...]),
            nn(act, grad_k[:span, :]),
            nn(act, grad_v[:span, :]),
        )
        for which, product in enumerate(products):
            lanes = slice(which * BLOCK, (which + 1) * BLOCK)
            if more:
                product = product + before_ref[0, :, lanes]
            if last:
                weights[:, lanes] = product
            else:
                outs[0][0, :, lanes] = product

    for span in SPANS:
        pl.when(place[1] == span)(functools.partial(work, span))
    own_share[...] += nt(grad_q[...], wq_ref[...])
    if last:
        cut = 2 * BLOCK + LANES
        first = jnp.concatenate([weights[:, :BLOCK], weights[:, 2 * BLOCK : cut]], axis=1)
        other = jnp.concatenate([weights[:, BLOCK : 2 * BLOCK], weights[:, cut:]], axis=1)
        part_rows(first, place[2], outs[0], outs[1])
        part_rows(other, place[2], outs[2], outs[3])

    @pl.when(group == pl.num_programs(0) - 1)
    def _():
        def piece(k):
            return share[pl.ds(pl.multiple_of((place[0] ^ k) * rows, rows), rows), :]

        keep_ref[0] = piece(0) + own_share[...]
        keep_ref[1] = piece(1)
        send_ref[0] = piece(2).astype(BF)
        send_ref[1] = piece(3).astype(BF)


def norm_back_kernel(
    s, parts, keep_ref, core_ref, near_ref, tok_ref, gres_ref, mod_ref, gain_ref, before_ref,
    grad_ref, send_ref, sums_ref,
):
    def add(row, value):
        sums_ref[row : row + 1, :] = before_ref[row : row + 1, :] + rows_sum(value)

    pull = keep_ref[0] + core_ref[0].astype(F32) + near_ref[...].astype(F32)
    normed, inverse = normalize(tok_ref[...].astype(F32))
    gain = gain_ref[...]
    sums_ref[...] = before_ref[...]
    add(s, pull)
    add(parts + s, pull * (normed * gain))
    scaled = pull * (1.0 + mod_ref[0, 1:2, :])
    add(sums_ref.shape[0] - 8, scaled * normed)
    grad = gres_ref[0] + norm_back(scaled * gain, normed, inverse)
    grad_ref[...] = grad
    send_ref[...] = grad.astype(BF)


def part_rows(value, core, keep_ref, send_ref):
    blocks, piece, columns = keep_ref.shape
    both = value.reshape(blocks, 2, piece, columns)
    keep_ref[...] = jnp.where(core == 0, both[:, 0], both[:, 1]).astype(keep_ref.dtype)
    send_ref[...] = jnp.where(core == 0, both[:, 1], both[:, 0]).astype(BF)


def combine_kernel(index, *refs):
    for which in range(2):
        mine, got, other, other_got = refs[4 * which : 4 * which + 4]
        keep_ref, send_ref = refs[8 + 2 * which : 10 + 2 * which]
        keep_ref[...] = (mine[...].astype(F32) + got[...].astype(F32)).astype(keep_ref.dtype)
        send_ref[...] = (other[...].astype(F32) + other_got[...].astype(F32)).astype(BF)


def spread_kernel(place, keep_a, got_a, keep_b, got_b, *out_refs):
    rows, wide = keep_a.shape[1:]
    columns = keep_b.shape[2]
    if len(out_refs) == 2:
        out_refs = (out_refs[0].at[0], out_refs[1].at[0], out_refs[0].at[1], out_refs[1].at[1])
    for turn, out_ref in enumerate(out_refs):
        at = place[0] ^ turn
        out_ref[:, :wide] = (keep_a[at].astype(F32) + got_a[at].astype(F32)).astype(out_ref.dtype)
        below = keep_b[at].astype(F32) + got_b[at].astype(F32)
        for k in range(keep_b.shape[1] // rows):
            lanes = slice(wide + k * columns, wide + (k + 1) * columns)
            out_ref[:, lanes] = below[k * rows : (k + 1) * rows].astype(out_ref.dtype)


def place_mlp_kernel(own_ref, near_ref, far_ref, up_ref, out_ref, down_ref):
    total = own_ref[0] + near_ref[0].astype(F32) + far_ref[...].astype(F32)
    rows, hidden = up_ref.shape
    width = out_ref.shape[1]
    up_ref[...] = total[:, :hidden]
    out_ref[...] = total[:, hidden : hidden + width]
    for k in range(down_ref.shape[0] // rows):
        at = hidden + (k + 1) * width
        down_ref[k * rows : (k + 1) * rows, :] = total[:, at : at + width]


def place_att_kernel(own_ref, near_ref, far_ref, qkv_ref):
    total = own_ref[0] + near_ref[0].astype(F32) + far_ref[...].astype(F32)
    width = qkv_ref.shape[1] // 3
    step, side = BLOCK + LANES, width // BLOCK * (BLOCK + LANES)
    for j in range(width // BLOCK):
        for which in range(2):
            at = which * side + j * step
            to = which * width + j * BLOCK
            qkv_ref[:, to : to + BLOCK] = total[:, at : at + BLOCK]
            to = 2 * width + j * BLOCK + which * LANES
            qkv_ref[:, to : to + LANES] = total[:, at + BLOCK : at + step]


def mlp_kernel(
    core, mix0_ref, mix1_ref, mix2_ref, tok_ref, cot_ref, mod_ref, gain_ref, wout_ref, bdown_ref,
    wup_ref, bup_ref, wdown_ref,
    out_ref, gres_ref, gmix_ref, sums_ref,
    keepup_ref, sendup_ref, keepdown_ref, senddown_ref,
    resid, branch, act, act_t, slope, active, second, gsecond, gact, gpre,
):
    step = pl.program_id(0)
    tiles = pl.num_programs(0) // 2
    parts, rows, _ = tok_ref.shape
    mixes = (mix0_ref, mix1_ref, mix2_ref)

    def span(s):
        return slice(s * rows, (s + 1) * rows)

    def mod(s, which):
        return mod_ref[s, which : which + 1, :]

    @pl.when(step == 0)
    def _():
        sums_ref[...] = jnp.zeros_like(sums_ref)
        for s in range(parts):
            one = nn(mixes[s][...], wout_ref[...])
            res = tok_ref[s].astype(F32) + mod(s, 2) * one
            branch[span(s), :] = one
            resid[span(s), :] = res
            normed, _ = normalize(res)
            value = (normed * gain_ref[...] * (1.0 + mod(s, 4)) + mod(s, 3)).astype(BF)
            act[span(s), :] = value
            act_t[:, span(s)] = value.T
            second[span(s), :] = jnp.zeros_like(res)
            gact[span(s), :] = jnp.zeros_like(res)

    @pl.when(step < tiles)
    def _():
        for s in range(parts):
            u = nn(act[span(s), :], wup_ref[...]) + bup_ref[...]
            square = u * u
            bent = jnp.tanh(GELU_C * (u + 0.044715 * (square * u)))
            value = (0.5 * u * (1.0 + bent)).astype(BF)
            slope[step, span(s), :] = 0.5 * (1.0 + bent) + 0.5 * u * (1.0 - bent * bent) * (
                GELU_C * (1.0 + 3 * 0.044715 * square)
            )
            active[step, span(s), :] = value
            second[span(s), :] += nn(value, wdown_ref[...])

    @pl.when(step == tiles - 1)
    def _():
        total = jnp.zeros(bdown_ref.shape, F32)
        for s in range(parts):
            two = second[span(s), :] + bdown_ref[...]
            out_ref[s] = (resid[span(s), :] + mod(s, 5) * two).astype(BF)
            pull = cot_ref[s].astype(F32)
            sums_ref[5 * parts + s : 5 * parts + s + 1, :] = rows_sum(pull * two)
            down = (pull * mod(s, 5)).astype(BF)
            gsecond[span(s), :] = down
            total = total + rows_sum(down.astype(F32))
        sums_ref[6 * parts : 6 * parts + 1, :] = total

    @pl.when((step >= tiles) & (step < 2 * tiles))
    def _():
        at = step - tiles
        total = jnp.zeros(bup_ref.shape, F32)
        for s in range(parts):
            pulled = nt(gsecond[span(s), :], wdown_ref[...])
            value = (pulled * slope[at, span(s), :]).astype(BF)
            gpre[span(s), :] = value
            total = total + rows_sum(value.astype(F32))
            gact[span(s), :] += nt(value, wup_ref[...])
        sums_ref[pl.ds(6 * parts + 2 + at, 1), :] = total
        part_rows(nn(active[at].T, gsecond[...]), core[0], keepdown_ref, senddown_ref)
        part_rows(nn(act_t[...], gpre[...]), core[0], keepup_ref, sendup_ref)

    @pl.when(step == 2 * tiles)
    def _():
        total = jnp.zeros(bdown_ref.shape, F32)
        outer = jnp.zeros(resid.shape[1:] * 2, F32)
        for s in range(parts):
            normed, inverse = normalize(resid[span(s), :])
            pull = gact[span(s), :]
            sums_ref[3 * parts + s : 3 * parts + s + 1, :] = rows_sum(pull)
            sums_ref[4 * parts + s : 4 * parts + s + 1, :] = rows_sum(
                pull * (normed * gain_ref[...])
            )
            scaled = pull * (1.0 + mod(s, 4))
            total = total + rows_sum(scaled * normed)
            grad = cot_ref[s].astype(F32) + norm_back(scaled * gain_ref[...], normed, inverse)
            gres_ref[s] = grad
            sums_ref[2 * parts + s : 2 * parts + s + 1, :] = rows_sum(grad * branch[span(s), :])
            one = (grad * mod(s, 2)).astype(BF)
            gmix_ref[s] = nt(one, wout_ref[...]).astype(BF)
            outer = outer + nn(mixes[s][...].T, one)
        part_rows(outer, core[0], keepup_ref, sendup_ref)
        sums_ref[6 * parts + 1 : 6 * parts + 2, :] = total


def whole(array):
    rank = array.ndim
    return pl.BlockSpec(array.shape, lambda *_: (0,) * rank, pipeline_mode=pl.Buffered(1))


def limits(mib=60):
    return pltpu.CompilerParams(vmem_limit_bytes=mib * 2**20)


def cost(flops, bytes_accessed):
    return pl.CostEstimate(
        flops=int(flops) // SCALE, bytes_accessed=int(bytes_accessed) // SCALE, transcendentals=0
    )


def arrange(lengths, tokens, cond):
    parts, rows, width = tokens.shape
    shapes = [jax.ShapeDtypeStruct((rows, width), BF)] * parts
    shapes.append(jax.ShapeDtypeStruct((8, cond.shape[1] + LANES), F32))
    return pl.pallas_call(
        arrange_kernel,
        grid_spec=pltpu.PrefetchScalarGridSpec(
            num_scalar_prefetch=1,
            grid=(1,),
            in_specs=[whole(tokens), whole(cond)],
            out_specs=[whole(v) for v in shapes] + [pl.BlockSpec(memory_space=pltpu.SMEM)],
        ),
        out_shape=shapes + [jax.ShapeDtypeStruct((2 * parts,), jnp.int32)],
        compiler_params=limits(32),
        cost_estimate=cost(1e6, 3e6),
        name="arrange",
    )(lengths, tokens, cond)


def arrange_pulls(order, pulls):
    parts, rows, width = pulls.shape
    shapes = [jax.ShapeDtypeStruct((rows, width), BF)] * parts
    return pl.pallas_call(
        arrange_pulls_kernel,
        grid_spec=pltpu.PrefetchScalarGridSpec(
            num_scalar_prefetch=1,
            grid=(1,),
            in_specs=[whole(pulls)],
            out_specs=[whole(v) for v in shapes],
        ),
        out_shape=shapes,
        compiler_params=limits(32),
        cost_estimate=cost(1e6, 3e6),
        name="arrange_pulls",
    )(order, pulls)


def put(order, value, moved, grads, moves):
    parts, rows, width = value.shape
    block = pl.BlockSpec((1, rows, width), lambda i, p: (i, 0, 0))
    placed = pl.BlockSpec((1, rows, width), lambda i, p: (p[i], 0, 0))
    return pl.pallas_call(
        put_kernel,
        grid_spec=pltpu.PrefetchScalarGridSpec(
            num_scalar_prefetch=1,
            grid=(parts,),
            in_specs=[block, block] + [whole(v) for v in list(grads) + list(moves)],
            out_specs=[placed, placed],
        ),
        out_shape=[
            jax.ShapeDtypeStruct(value.shape, BF),
            jax.ShapeDtypeStruct(value.shape, F32),
        ],
        compiler_params=limits(),
        cost_estimate=cost(1e6, 1e7),
        name="put",
    )(order, value, moved, *grads, *moves)


def prepare(place, pieces, mod, s, gain, w_qkv, cosine, sine):
    rows, width = pieces[0].shape
    slots = 4 * rows
    table = pl.BlockSpec((rows, LANES), lambda i, p: (p[0] ^ i, 0))
    piece = pl.BlockSpec((rows, width), lambda i, p: (p[0] ^ i, 0))
    return pl.pallas_call(
        prep_kernel,
        grid_spec=pltpu.PrefetchScalarGridSpec(
            num_scalar_prefetch=1,
            grid=(4,),
            in_specs=[whole(a) for a in pieces]
            + [pl.BlockSpec((1,) + mod.shape[1:], lambda i, p: (s, 0, 0))]
            + [whole(gain), whole(w_qkv), table, table],
            out_specs=[
                pl.BlockSpec((width, rows), lambda i, p: (0, p[0] ^ i)),
                pl.BlockSpec((rows, width), lambda i, p: (0, 0)),
                piece, piece,
            ],
        ),
        out_shape=[
            jax.ShapeDtypeStruct((width, slots), BF),
            jax.ShapeDtypeStruct((rows, width), BF),
            jax.ShapeDtypeStruct((slots, width), BF),
            jax.ShapeDtypeStruct((slots, width), BF),
        ],
        compiler_params=limits(32),
        cost_estimate=cost(2 * slots * width * width * 2.25, 10e6),
        name="prepare",
    )(place, *pieces, mod, gain, w_qkv, cosine, sine)


def attend(place, queries, keys, values):
    rows, width = queries.shape
    slots = keys.shape[0]
    groups = width // BLOCK
    own = pl.BlockSpec((rows, BLOCK), lambda j, p: (0, j))
    full = pl.BlockSpec((slots, BLOCK), lambda j, p: (0, j))
    return pl.pallas_call(
        attend_kernel,
        grid_spec=pltpu.PrefetchScalarGridSpec(
            num_scalar_prefetch=1,
            grid=(groups,),
            in_specs=[own, full, full],
            out_specs=[own, pl.BlockSpec((1, 8, rows), lambda j, p: (j, 0, 0))],
        ),
        out_shape=[
            jax.ShapeDtypeStruct((rows, width), BF),
            jax.ShapeDtypeStruct((groups, 8, rows), F32),
        ],
        compiler_params=limits(32),
        cost_estimate=cost(16 * rows * slots * width, 5e6),
        name="attend",
    )(place, queries, keys, values)


def attend_back(
    place, queries, keys, values, grads, s, logs, cosine, sine, w_qkv, act_t, before, last, dp_size
):
    rows, width = queries.shape
    slots = keys.shape[0]
    groups = width // BLOCK
    own = pl.BlockSpec((rows, BLOCK), lambda j, p: (0, j))
    full = pl.BlockSpec((slots, BLOCK), lambda j, p: (0, j))
    own_table = pl.BlockSpec((rows, LANES), lambda j, p: (p[0], 0))
    full_table = pl.BlockSpec((slots, LANES), lambda j, p: (0, 0))
    every = pl.BlockSpec((1, width, 3 * BLOCK), lambda j, p: (j, 0, 0))
    blocks, piece, columns = dp_size // 2, width // dp_size, BLOCK + LANES
    more = before is not None
    if last:
        part = (blocks, piece, groups * columns)
        weight_specs = [pl.BlockSpec((blocks, piece, columns), lambda j, p: (0, 0, j))] * 4
        weight_shapes = [jax.ShapeDtypeStruct(part, F32), jax.ShapeDtypeStruct(part, BF)] * 2
    else:
        weight_specs = [every]
        weight_shapes = [jax.ShapeDtypeStruct((groups, width, 3 * BLOCK), F32)]
    return pl.pallas_call(
        functools.partial(attend_back_kernel, more, last),
        grid_spec=pltpu.PrefetchScalarGridSpec(
            num_scalar_prefetch=1,
            grid=(groups,),
            in_specs=[
                own, full, full,
                pl.BlockSpec((None, rows, BLOCK), lambda j, p: (s, 0, j)),
                pl.BlockSpec((1, 8, rows), lambda j, p: (j, 0, 0)),
                own_table, own_table, full_table, full_table,
                pl.BlockSpec((width, BLOCK), lambda j, p: (0, j)),
                pl.BlockSpec((width, BLOCK), lambda j, p: (0, groups + j)),
                pl.BlockSpec((width, BLOCK), lambda j, p: (0, 2 * groups + j)),
                whole(act_t),
                pl.BlockSpec((width, rows), lambda j, p: (0, p[0])),
            ]
            + [every] * more,
            out_specs=[pl.BlockSpec((2, rows, width), lambda j, p: (0, 0, 0))] * 2 + weight_specs,
            scratch_shapes=[
                pltpu.VMEM((slots, width), F32),
                pltpu.VMEM((rows, width), F32),
                pltpu.VMEM((rows, BLOCK), BF),
                pltpu.VMEM((slots, BLOCK), BF),
                pltpu.VMEM((slots, BLOCK), BF),
                pltpu.VMEM((width, 3 * BLOCK), F32),
            ],
        ),
        out_shape=[
            jax.ShapeDtypeStruct((2, rows, width), F32),
            jax.ShapeDtypeStruct((2, rows, width), BF),
        ]
        + weight_shapes,
        compiler_params=limits(),
        cost_estimate=cost(60 * rows * slots * width, 12e6),
        name="attend_back",
    )(
        place, queries, keys, values, grads, logs, cosine, sine, cosine, sine, w_qkv, w_qkv,
        w_qkv, act_t, act_t, *([before] if more else []),
    )


def norm_one_back(keep, core_got, near_got, tokens, grad_res, s, mod, gain, sums):
    rows, width = tokens.shape
    first = pl.BlockSpec((1, rows, width), lambda i: (0, 0, 0))
    return pl.pallas_call(
        functools.partial(norm_back_kernel, s, mod.shape[0]),
        grid=(1,),
        in_specs=[
            first, first, whole(near_got), whole(tokens),
            pl.BlockSpec((1, rows, width), lambda i: (s, 0, 0)),
            pl.BlockSpec((1,) + mod.shape[1:], lambda i: (s, 0, 0)),
            whole(gain), whole(sums),
        ],
        out_specs=[pl.BlockSpec((rows, width), lambda i: (0, 0))] * 2
        + [pl.BlockSpec(sums.shape, lambda i: (0, 0))],
        out_shape=[
            jax.ShapeDtypeStruct((rows, width), F32),
            jax.ShapeDtypeStruct((rows, width), BF),
            jax.ShapeDtypeStruct(sums.shape, F32),
        ],
        compiler_params=limits(),
        cost_estimate=cost(40 * rows * width, 6e6),
        name="norm_one_back",
    )(keep, core_got, near_got, tokens, grad_res, mod, gain, sums)


def feed_forward(core, mixes, tokens, pulls, mod, gain, w_out, b_down, w_up, b_up, w_down, dp_size):
    parts, rows, width = tokens.shape
    hidden = w_up.shape[1]
    tile = width
    tiles = hidden // tile
    total = parts * rows
    blocks, piece = dp_size // 2, width // dp_size
    tall_piece = hidden // dp_size
    per_tile = tile // (2 * tall_piece)
    late = lambda i: jnp.maximum(i - tiles, 0)
    last = lambda i: jnp.minimum(late(i), tiles - 1)
    turn = lambda i: jnp.minimum(jnp.where(i < tiles, i, i - tiles), tiles - 1)
    wide = pl.BlockSpec((width, tile), lambda i, c: (0, turn(i)))
    bias = pl.BlockSpec((1, tile), lambda i, c: (0, turn(i)))
    tall = pl.BlockSpec((tile, width), lambda i, c: (turn(i), 0))
    out_wide = pl.BlockSpec((blocks, piece, tile), lambda i, c: (0, 0, late(i)))
    out_tall = pl.BlockSpec((per_tile, tall_piece, width), lambda i, c: (last(i), 0, 0))
    outs = [
        jax.ShapeDtypeStruct(tokens.shape, BF),
        jax.ShapeDtypeStruct(tokens.shape, F32),
        jax.ShapeDtypeStruct(tokens.shape, BF),
        jax.ShapeDtypeStruct((6 * parts + 2 + hidden // width + 8, width), F32),
        jax.ShapeDtypeStruct((blocks, piece, hidden + width), BF),
        jax.ShapeDtypeStruct((blocks, piece, hidden + width), BF),
        jax.ShapeDtypeStruct((blocks, tall_piece, width), BF),
        jax.ShapeDtypeStruct((blocks, tall_piece, width), BF),
    ]
    return pl.pallas_call(
        mlp_kernel,
        grid_spec=pltpu.PrefetchScalarGridSpec(
            num_scalar_prefetch=1,
            grid=(2 * tiles + 1,),
            in_specs=[whole(m) for m in mixes]
            + [whole(a) for a in (tokens, pulls, mod, gain, w_out, b_down)]
            + [wide, bias, tall],
            out_specs=[whole(o) for o in outs[:4]]
            + [out_wide, out_wide, out_tall, out_tall],
            scratch_shapes=[
                pltpu.VMEM((total, width), F32),
                pltpu.VMEM((total, width), F32),
                pltpu.VMEM((total, width), BF),
                pltpu.VMEM((width, total), BF),
                pltpu.VMEM((tiles, total, tile), F32),
                pltpu.VMEM((tiles, total, tile), BF),
                pltpu.VMEM((total, width), F32),
                pltpu.VMEM((total, width), BF),
                pltpu.VMEM((total, width), F32),
                pltpu.VMEM((total, tile), BF),
            ],
        ),
        out_shape=outs,
        compiler_params=limits(),
        cost_estimate=cost(2 * total * width * (6 * hidden + 3 * width), 50e6),
        name="feed_forward",
    )(core, *mixes, tokens, pulls, mod, gain, w_out, b_down, w_up, b_up, w_down)


def combine(index, streams, turns, kept):
    in_specs, out_specs, shapes, inputs = [], [], [], []
    for which, (keep, got) in enumerate(streams):
        above, _, below, rows, columns = keep.shape
        tile = columns // turns
        block = (None, None, None, rows, tile)

        def place(i, c, p, flip, which=which, below=below):
            return (i // below, 1 - p[which] if flip else p[which], i % below, 0, c)

        mine = pl.BlockSpec(block, functools.partial(place, flip=False))
        other = pl.BlockSpec(block, functools.partial(place, flip=True))
        out = pl.BlockSpec((None, rows, tile), lambda i, c, p: (i, 0, c))
        in_specs += [mine, mine, other, other]
        inputs += [keep, got, keep, got]
        out_specs += [out, out]
        shape = (above * below, rows, columns)
        shapes += [jax.ShapeDtypeStruct(shape, kept), jax.ShapeDtypeStruct(shape, BF)]
        steps = above * below
    return pl.pallas_call(
        combine_kernel,
        grid_spec=pltpu.PrefetchScalarGridSpec(
            num_scalar_prefetch=1, grid=(steps, turns), in_specs=in_specs, out_specs=out_specs
        ),
        out_shape=shapes,
        compiler_params=limits(),
        cost_estimate=cost(inputs[0].size * 4, inputs[0].size * 18),
        name="combine",
    )(index, *inputs)


def spread(place, keep_a, got_a, keep_b, got_b, paired):
    _, rows, wide = keep_a.shape
    columns = wide + keep_b[0].size // rows
    if paired:
        shapes = [jax.ShapeDtypeStruct((2, rows, columns), t) for t in (F32, BF)]
    else:
        shapes = [jax.ShapeDtypeStruct((rows, columns), t) for t in (F32, BF, BF, BF)]
    arrays = (keep_a, got_a, keep_b, got_b)
    return pl.pallas_call(
        spread_kernel,
        grid_spec=pltpu.PrefetchScalarGridSpec(
            num_scalar_prefetch=1,
            grid=(1,),
            in_specs=[whole(v) for v in arrays],
            out_specs=[whole(v) for v in shapes],
        ),
        out_shape=shapes,
        compiler_params=limits(),
        cost_estimate=cost(columns * rows * 8, columns * rows * 40),
        name="spread",
    )(place, *arrays)


def place_weights(kernel, own, near, far, shapes):
    return pl.pallas_call(
        kernel,
        grid=(1,),
        in_specs=[pl.BlockSpec((1,) + far.shape, lambda i: (0, 0, 0))] * 2 + [whole(far)],
        out_specs=[whole(v) for v in shapes],
        out_shape=shapes,
        compiler_params=limits(),
        cost_estimate=cost(far.size * 2, far.size * 12),
        name="place_weights",
    )(own, near, far)


def after(value, *others):
    return lax.optimization_barrier((value,) + others)[0]


def body(
    dp_size, seq_size,
    tokens, cond, lengths, gain_one, gain_two, w_ada, b_ada, w_qkv, w_out, w_up, b_up, w_down,
    b_down, cotangent,
):
    parts, rows, width = tokens.shape
    hidden = w_up.shape[1]
    slots = rows * seq_size
    dp_bits = dp_size.bit_length() - 1
    dp, seq = lax.axis_index("dp").astype(jnp.int32), lax.axis_index("seq").astype(jnp.int32)
    core, side = dp & 1, lax.shift_right_logical(seq, jnp.int32(seq_size.bit_length() - 2))
    stays = core == side
    own = jnp.where(stays, seq, seq ^ 2).astype(jnp.int32)

    def dp_swap(value, bit):
        return lax.ppermute(value, "dp", [(i, i ^ (1 << bit)) for i in range(dp_size)])

    def seq_swap(value, bit):
        return lax.ppermute(value, "seq", [(i, i ^ (1 << bit)) for i in range(seq_size)])

    def swap(value, axis, bit):
        return dp_swap(value, bit) if axis == "dp" else seq_swap(value, bit)

    def bit_of(axis, bit):
        return ((dp if axis == "dp" else seq) >> bit) & 1

    pairs = []
    for i in range(dp_size):
        for j in range(seq_size):
            if (i & 1) != j // (seq_size // 2):
                pairs.append((i * seq_size + j, (i ^ 1) * seq_size + (j ^ 2)))

    def send_across(value):
        return lax.ppermute(value, ("dp", "seq"), pairs)

    def settle(value, moved, *others):
        return jnp.where(stays, value, after(moved, *others).astype(value.dtype))

    def regroup(value, moving=None):
        return settle(value, send_across(value if moving is None else moving))

    *sorted_tokens, both, order = arrange(lengths, tokens, cond.astype(F32))

    puts = jnp.concatenate([order[:parts], stays.astype(jnp.int32)[None]])

    mine = [None] * parts
    mine[0] = regroup(sorted_tokens[0])
    both = jnp.where(stays, both, dp_swap(both, 0))
    cond_here, lengths_here = both[:parts, :-LANES].astype(BF), both[:, -1].astype(jnp.int32)
    mod = jnp.dot(cond_here, w_ada, preferred_element_type=F32) + b_ada
    mod = mod.reshape(parts, 6, width)
    places = [jnp.stack([own, lengths_here[s], core]).astype(jnp.int32) for s in range(parts)]
    core_index = core.astype(jnp.int32)[None]
    frequency = np.power(10000.0, -np.arange(HD // 2) * 2.0 / HD).astype(np.float32)
    angles = np.arange(slots).astype(np.float32)[:, None] * frequency[None, :]
    angles = angles.astype(np.float64)
    cosine = jnp.asarray(np.tile(np.cos(angles), (1, LANES // (HD // 2))).astype(np.float32))
    sine = np.sin(angles)
    sine = jnp.asarray(np.tile(np.concatenate([-sine, sine], 1), (1, LANES // HD)).astype(np.float32))
    gain_one_row, gain_two_row = gain_one[None, :], gain_two[None, :]

    saved, mixes = [], []
    tie = lax.optimization_barrier
    forth = list(range(1, dp_bits))
    back = forth[::-1]
    halves = [jnp.stack([bit_of("dp", i), bit_of("dp", j)]) for i, j in zip(forth, back)]
    own_seq = seq[None]
    mine[0] = after(mine[0], mod, *places, *halves, own_seq, puts, core_index)
    nears = [seq_swap(mine[0], 0)]
    moving = send_across(after(sorted_tokens[1], mine[0]))
    fars = [dp_swap(mine[0], 0)]
    mine[1] = settle(sorted_tokens[1], moving)
    nears.append(seq_swap(mine[1], 0))
    if parts > 2:
        moving = send_across(after(sorted_tokens[2], mine[1]))
    pulls, pulled = arrange_pulls(order, after(cotangent, mine[0])), []
    for s in range(parts):
        group = (mine[s], nears[s], fars[s], dp_swap(nears[s], 0))
        group = tie((group, mixes[-1] if s else mine[1], tuple(pulled) if s > 1 else ()))[0]
        if s == parts - 1:
            pulled += [send_across(after(pulls[k], nears[s])) for k in range(len(pulled), parts)]
        act_t, queries, keys, values = prepare(
            places[s], group, mod, s, gain_one_row, w_qkv, cosine, sine
        )
        if s == parts - 1:
            queries = after(queries, *pulled)
        mixture, logs = attend(places[s], queries, keys, values)
        saved.append((act_t, queries, keys, values, logs))
        mixes.append(mixture)
        if s + 1 < parts:
            nears[s + 1] = after(nears[s + 1], mixture)
            fars.append(dp_swap(after(mine[s + 1], mixture), 0))
        if s + 2 < parts:
            mine[s + 2] = settle(sorted_tokens[s + 2], moving, mixture)
            nears.append(seq_swap(mine[s + 2], 0))
            if s == 0:
                pulled += [send_across(after(pulls[k], mine[2])) for k in range(parts - 1)]
            if s + 3 < parts:
                moving = send_across(after(sorted_tokens[s + 3], mine[s + 2]))
    pulls = [settle(v, m, mixes[-1]) for v, m in zip(pulls, pulled)]

    output, grad_res, grad_mix, sums, keep_up, send_up, keep_down, send_down = feed_forward(
        core_index, mixes, jnp.stack(mine), jnp.stack(pulls), mod, gain_two_row, w_out,
        b_down[None, :], w_up, b_up[None, :], w_down, dp_size,
    )
    output_moved = send_across(output)

    class Halving:
        def __init__(self, arrays, sends, turns):
            self.arrays, self.sends, self.turns, self.at = arrays, sends, turns, [0, 0]
            self.orders = [list(forth), list(back)]
            self.names = [forth[::-1], forth[::-1]]
            self.move()

        def merge(self, kept=F32):
            streams, self.at = [], []
            index = halves[len(forth) - len(self.orders[0])]
            for which in range(2):
                bit = self.orders[which].pop(0)
                names = self.names[which]
                place = names.index(bit)
                names.pop(place)
                keep = self.arrays[which]
                shape = (2**place, 2, 2 ** (len(names) - place)) + keep.shape[1:]
                streams.append((keep.reshape(shape), self.got[which].reshape(shape)))
                self.at.append(bit)
            keep_a, send_a, keep_b, send_b = combine(index, streams, self.turns, kept)
            self.arrays, self.sends, self.turns = [keep_a, keep_b], [send_a, send_b], 1
            return self.sends

        def move(self):
            self.got = [dp_swap(v, bit) for v, bit in zip(self.sends, self.at)]

        def spread(self, paired):
            pieces = [
                v.reshape(seq_size, v.shape[1] // seq_size, v.shape[2]) for v in self.arrays + self.got
            ]
            self.own, *self.sends = spread(
                own_seq, pieces[0], pieces[2], pieces[1], pieces[3], paired
            )
            return self.sends

        def send(self):
            self.got = [
                lax.ppermute(v, "seq", [(i, i ^ k) for i in range(seq_size)])
                for k, v in enumerate(self.sends, 1)
            ]

    mlp = Halving([keep_up, keep_down], [send_up, send_down], 3)

    shares, cores, nears, grad_tokens, moved = [], [], [], [], []

    def pass_on(s):
        there = (shares[s][0][1] + cores[s][1].astype(F32)).astype(BF)
        nears.append(seq_swap(there, 0))
        return there

    def finish(s, sums):
        grad, rounded, sums = norm_one_back(
            shares[s][0], cores[s], nears[s], mine[s], grad_res, s, mod, gain_one_row, sums
        )
        grad_tokens.append(grad)
        return rounded, sums

    def give_back(s, rounded):
        moved.append(send_across(rounded))

    waits, weights = [], [None]
    for s in range(parts):
        act_t, queries, keys, values, logs = saved[s]
        keep, send, *weights = attend_back(
            places[s], after(queries, *waits), keys, values, grad_mix, s, logs, cosine,
            sine, w_qkv, act_t, weights[0], s == parts - 1, dp_size,
        )
        if s == 0:
            send, weights, mlp.got = tie((send, weights, mlp.got))
        elif s == 1:
            send, weights, mlp.got, nears[0], output_moved = tie(
                (send, weights, mlp.got, nears[0], output_moved)
            )
        else:
            send, weights, mlp.got, nears[1], moved[0] = tie(
                (send, weights, mlp.got, nears[1], moved[0])
            )
        shares.append((keep, send))
        cores.append(dp_swap(send, 0))
        if s == parts - 1:
            break
        if mlp.orders[0]:
            waits = list(mlp.merge(BF if s == 0 else F32))
            mlp.move()
        if s:
            rounded, sums = finish(s - 1, sums)
            give_back(s - 1, rounded)
            waits.append(rounded)
        waits.append(pass_on(s))

    while mlp.orders[0]:
        mlp.merge()
        mlp.move()
    att = Halving([weights[0], weights[2]], [weights[1], weights[3]], 1)
    rounded, sums = finish(parts - 2, sums)
    cores[-1] = after(cores[-1], rounded)
    passed = pass_on(parts - 1)
    give_back(parts - 2, after(rounded, passed))
    att.got = tie((att.got, passed))[0]
    waits = att.merge()
    att.move()
    mlp.got = tie((mlp.got, *waits))[0]
    waits = mlp.spread(True)
    nears[-1], mlp.sends = tie((nears[-1], mlp.sends, *waits))[:2]
    mlp.send()
    rounded, sums = finish(parts - 1, sums)
    across = dp_swap(sums, 0)
    give_back(parts - 1, rounded)
    waits = [rounded]
    while att.orders[0]:
        att.got = tie((att.got, *waits))[0]
        waits = att.merge()
        att.move()
    held = sums + after(across, *waits)
    across = seq_swap(held, 0)
    mlp.got, moved[-2] = tie((mlp.got, moved[-2], held))[:2]
    further = (mlp.own[1] + mlp.got[0][1].astype(F32)).astype(BF)
    att.got = tie((att.got, further))[0]
    waits = att.spread(True)
    held = held + after(across, *waits)
    att.send()
    further = seq_swap(further, 1)
    count, kept = 6 * parts, held.shape[0] - 7
    conds = cond_here.astype(F32).reshape(1, -1)
    conds = jnp.pad(conds, ((0, 0), (0, width - conds.shape[1])))
    ours = jnp.concatenate([held[:kept], conds]).astype(BF)[None]
    got = swap(ours, "seq", 1)
    mod_here = jnp.where(stays, held[:count], got[0, :count].astype(F32))
    ours = jnp.concatenate([ours, got])
    for bit in forth:
        got = swap(ours, "dp", bit)
        if bit == forth[0]:
            att.got = tie((att.got, ours))[0]
            later = (att.own[1] + att.got[0][1].astype(F32)).astype(BF)
            got = after(got, later)
            later = seq_swap(later, 1)
        ours = jnp.concatenate([ours, got])
    ours = ours.astype(F32)
    totals = jnp.sum(ours[:, count:kept], axis=0)
    output, g_tokens = put(puts, output, output_moved, grad_tokens, tie((tuple(moved), ours))[0])
    piece = width // (dp_size * seq_size)
    tall = hidden // (dp_size * seq_size)
    shapes = [
        jax.ShapeDtypeStruct((piece, hidden), F32),
        jax.ShapeDtypeStruct((piece, width), F32),
        jax.ShapeDtypeStruct((tall, width), F32),
    ]
    g_w_up, g_w_out, g_w_down = place_weights(
        place_mlp_kernel, mlp.own, mlp.got[0], after(further, g_tokens), shapes
    )
    shapes = [jax.ShapeDtypeStruct((piece, 3 * width), F32)]
    (g_w_qkv,) = place_weights(
        place_att_kernel, att.own, att.got[0], after(later, g_w_out), shapes
    )

    w_ada_f = w_ada.astype(F32)
    g_cond = sum(
        jnp.dot(
            mod_here[k * parts : (k + 1) * parts],
            w_ada_f[:, k * width : (k + 1) * width].T,
            precision=HIGH,
        )
        for k in range(6)
    )
    chosen = order[:parts, None] == jnp.arange(parts)[None, :]
    g_cond = jnp.sum(jnp.where(chosen[:, :, None], g_cond[:, None], 0.0), axis=0)
    groups = ours.shape[0]
    conds = ours[:, kept, : cond_here.size].reshape(groups * parts, -1)
    lanes = ours[:, :count].reshape(groups, 6, parts, width).transpose(0, 2, 1, 3)
    lanes = lanes.reshape(groups * parts, 6 * width)
    shards = dp_size * seq_size
    index = dp * seq_size + seq

    def mine_of(value):
        size = value.shape[-1] // shards
        starts = (jnp.int32(0),) * (value.ndim - 1) + (index * size,)
        sizes = value.shape[:-1] + (size,)
        return lax.dynamic_slice(value, starts, sizes, allow_negative_indices=False)

    lanes = mine_of(lanes)
    g_w_ada = jnp.dot(conds.T, lanes, precision=HIGH)
    g_b_ada = jnp.sum(lanes, axis=0)
    g_b_down, g_gain_two, g_gain_one = mine_of(totals[0]), mine_of(totals[1]), mine_of(totals[-1])
    g_b_up = mine_of(totals[2:-1].reshape(-1))
    return (
        output,
        g_tokens,
        g_cond,
        g_gain_one,
        g_gain_two,
        g_w_ada,
        g_b_ada,
        g_w_qkv,
        g_w_out,
        g_w_up,
        g_b_up,
        g_w_down,
        g_b_down,
    )


def solution(mesh):
    shards = ("dp", "seq")
    placed = (
        (P("dp", "seq", None), P("dp", None), P("dp"))
        + (P(),) * 10
        + (P("dp", "seq", None),)
    )
    return jax.shard_map(
        functools.partial(body, mesh.shape["dp"], mesh.shape["seq"]),
        mesh=mesh,
        in_specs=placed,
        out_specs=(
            P("dp", "seq", None),
            P("dp", "seq", None),
            P("dp", None),
            P(shards),
            P(shards),
            P(None, shards),
            P(shards),
            P(shards, None),
            P(shards, None),
            P(shards, None),
            P(shards),
            P(shards, None),
            P(shards),
        ),
        check_vma=False,
    )
```

profile of v0, /device:TPU:0, one launch (start us, length us, event | category | flops | bytes accessed | tf_op | source)
XLA Modules:
  0.0 343.4 jit_solution(12871411062798924248)
XLA Ops:
  17.6 2.6 collective-permute-start.2
  20.9 8.4 %collective-permute-start.3 = (bf16[256,768]{1,0:T(8,128)(2,1)S(1)}, bf16[256,768]{1,0:T(8,128)(2,1)S(1)}, u32[]{:S(2)}, u32[]{:S(2)}) collective-permute-start(bf16[256,768]{1,0:T(8,128)(2,1)S(1)} %broadcast_select_fusion.2.a_ref.tok_ref), channel_id=1, source_target_pairs={{0,4},{4,0},{8,12},{12,8},{16,20},{20,16},{24,28},{28,24},{1,5},{5... | collective-permute-start | bytes 1179656 | tf_op jit(solution)/shard_map/ppermute | solution.py:788
  36.1 4.7 %prepare.3 = (bf16[768,1024]{1,0:T(8,128)(2,1)S(1)}, bf16[256,768]{1,0:T(8,128)(2,1)S(1)}, bf16[1024,768]{1,0:T(8,128)(2,1)S(1)}, bf16[1024,768]{1,0:T(8,128)(2,1)S(1)}) custom-call(s32[3]{0:T(128)S(1)} %add_add_fusion.place, bf16[256,768]{1,0:T(8,128)(2,1)S(1)} %broadcast_select_fusion.2.a_ref.tok_ref, bf16[256,768]{1,0:T(8,128)(2,1)S(1)} %collective-permute-done.2.b_ref, ...), custom_call_target="tpu_custom_call" | custom-call | flops 2717908 | bytes 10000 | tf_op jit(solution)/shard_map/prepare/pallas_call | solution.py:509
  42.0 5.2 %attend.3 = (bf16[256,768]{1,0:T(8,128)(2,1)S(1)}, f32[3,8,256]{2,1,0:T(8,128)S(1)}) custom-call(s32[3]{0:T(128)S(1)} %add_add_fusion.place, bf16[256,768]{1,0:T(8,128)(2,1)S(1)} %get-tuple-element.175.q_ref, bf16[1024,768]{1,0:T(8,128)(2,1)S(1)} %get-tuple-element.176.k_ref, bf16[1024,768]{1,0:T(8,128)(2,1)S(1)} %get-tuple-element.177.v_ref), custom_call_target="tpu_custom_call" | custom-call | flops 3221225 | bytes 5000 | tf_op jit(solution)/shard_map/attend/pallas_call | solution.py:541
  47.3 10.2 %collective-permute-start.7 = (bf16[256,768]{1,0:T(8,128)(2,1)S(1)}, bf16[256,768]{1,0:T(8,128)(2,1)S(1)}, u32[]{:S(2)}, u32[]{:S(2)}) collective-permute-start(bf16[256,768]{1,0:T(8,128)(2,1)S(1)} %broadcast_select_fusion.1.a_ref.tok_ref), channel_id=1, source_target_pairs={{0,4},{4,0},{8,12},{12,8},{16,20},{20,16},{24,28},{28,24},{1,5},{5... | collective-permute-start | bytes 1179656 | tf_op jit(solution)/shard_map/ppermute | solution.py:788
  60.0 4.7 %prepare.4 = (bf16[768,1024]{1,0:T(8,128)(2,1)S(1)}, bf16[256,768]{1,0:T(8,128)(2,1)S(1)}, bf16[1024,768]{1,0:T(8,128)(2,1)S(1)}, bf16[1024,768]{1,0:T(8,128)(2,1)S(1)}) custom-call(s32[3]{0:T(128)S(1)} %add_add_fusion.1.place, bf16[256,768]{1,0:T(8,128)(2,1)S(1)} %broadcast_select_fusion.1.a_ref.tok_ref, bf16[256,768]{1,0:T(8,128)(2,1)S(1)} %collective-permute-done.6.b_ref, ...), custom_call_target="tpu_custom_call" | custom-call | flops 2717908 | bytes 10000 | tf_op jit(solution)/shard_map/prepare/pallas_call | solution.py:509
  64.8 5.2 %attend.4 = (bf16[256,768]{1,0:T(8,128)(2,1)S(1)}, f32[3,8,256]{2,1,0:T(8,128)S(1)}) custom-call(s32[3]{0:T(128)S(1)} %add_add_fusion.1.place, bf16[256,768]{1,0:T(8,128)(2,1)S(1)} %get-tuple-element.229.q_ref, bf16[1024,768]{1,0:T(8,128)(2,1)S(1)} %get-tuple-element.186.k_ref, bf16[1024,768]{1,0:T(8,128)(2,1)S(1)} %get-tuple-element.187.v_ref), custom_call_target="tpu_custom_call" | custom-call | flops 3221225 | bytes 5000 | tf_op jit(solution)/shard_map/attend/pallas_call | solution.py:541
  72.4 5.0 %collective-permute-start.11 = (bf16[256,768]{1,0:T(8,128)(2,1)S(1)}, bf16[256,768]{1,0:T(8,128)(2,1)S(1)}, u32[]{:S(2)}, u32[]{:S(2)}) collective-permute-start(bf16[256,768]{1,0:T(8,128)(2,1)S(1)} %broadcast_select_fusion.a_ref.tok_ref), channel_id=1, source_target_pairs={{0,4},{4,0},{8,12},{12,8},{16,20},{20,16},{24,28},{28,24},{1,5},{5... | collective-permute-start | bytes 1179656 | tf_op jit(solution)/shard_map/ppermute | solution.py:788
  80.5 4.7 %prepare.5 = (bf16[768,1024]{1,0:T(8,128)(2,1)S(1)}, bf16[256,768]{1,0:T(8,128)(2,1)S(1)}, bf16[1024,768]{1,0:T(8,128)(2,1)S(1)}, bf16[1024,768]{1,0:T(8,128)(2,1)S(1)}) custom-call(s32[3]{0:T(128)S(1)} %add_add_fusion.2.place, bf16[256,768]{1,0:T(8,128)(2,1)S(1)} %broadcast_select_fusion.a_ref.tok_ref, bf16[256,768]{1,0:T(8,128)(2,1)S(1)} %collective-permute-done.10.b_ref, ...), custom_call_target="tpu_custom_call" | custom-call | flops 2717908 | bytes 10000 | tf_op jit(solution)/shard_map/prepare/pallas_call | solution.py:509
  85.3 5.2 %attend.5 = (bf16[256,768]{1,0:T(8,128)(2,1)S(1)}, f32[3,8,256]{2,1,0:T(8,128)S(1)}) custom-call(s32[3]{0:T(128)S(1)} %add_add_fusion.2.place, bf16[256,768]{1,0:T(8,128)(2,1)S(1)} %get-tuple-element.249.q_ref, bf16[1024,768]{1,0:T(8,128)(2,1)S(1)} %get-tuple-element.207.k_ref, bf16[1024,768]{1,0:T(8,128)(2,1)S(1)} %get-tuple-element.208.v_ref), custom_call_target="tpu_custom_call" | custom-call | flops 3221225 | bytes 5000 | tf_op jit(solution)/shard_map/attend/pallas_call | solution.py:541
  93.8 41.6 %feed_forward.1 = (bf16[3,256,768]{2,1,0:T(8,128)(2,1)}, f32[3,256,768]{2,1,0:T(8,128)}, bf16[3,256,768]{2,1,0:T(8,128)(2,1)}, f32[32,768]{1,0:T(8,128)}, bf16[4...) custom-call(s32[1]{0:T(128)} %bitcast.1.core, ...), custom_call_target="tpu_custom_call" | custom-call | flops 24461180 | bytes 50000 | tf_op jit(solution)/shard_map/feed_forward/pallas_call | solution.py:672
  135.4 6.8 %collective-permute-start.16 = (bf16[4,96,3840]{2,1,0:T(8,128)(2,1)}, bf16[4,96,3840]{2,1,0:T(8,128)(2,1)S(1)}, u32[]{:S(2)}, u32[]{:S(2)}) collective-permute-start(bf16[4,96,3840]{2,1,0:T(8,128)(2,1)} %get-tuple-element.220), channel_id=1, source_target_pairs={{0,4},{4,0},{8,12},{12,8},{16,20},{20,16},{24,28},{28,24},{1,5},{5... | collective-permute-start | bytes 8847368 | tf_op jit(solution)/shard_map/ppermute | solution.py:788
  142.3 15.9 %attend_back.3 = (f32[2,256,768]{2,1,0:T(8,128)}, bf16[2,256,768]{2,1,0:T(8,128)(2,1)}, f32[3,768,768]{2,1,0:T(8,128)}) custom-call(s32[3]{0:T(128)} %copy-done.35, bf16[256,768]{1,0:T(8,128)(2,1)} %copy-done.20, bf16[1024,768]{1,0:T(8,128)(2,1)} %copy-done.12, bf16[1024,768]{1,0:T(8,128)(2,1)} %copy-done.13, bf16[3,256,768]{2,1,0:T(8,128)(2,1)} %get-tuple-element.215.g_ref, ...), custom_call_target="tpu_custom_call" | custom-call | flops 12079595 | bytes 12000 | tf_op jit(solution)/shard_map/attend_back/pallas_call | solution.py:579
  159.8 8.4 %combine.4 = (bf16[2,96,3840]{2,1,0:T(8,128)(2,1)}, bf16[2,96,3840]{2,1,0:T(8,128)(2,1)}, bf16[2,384,768]{2,1,0:T(8,128)(2,1)}, bf16[2,384,768]{2,1,0:T(8,128)(2,1)}) custom-call(s32[2]{0:T(128)} %pad_add_fusion.1.index, bf16[2,2,1,96,3840]{4,3,2,1,0:T(8,128)(2,1)} %bitcast.94, bf16[2,2,1,96,3840]{4,3,2,1,0:T(8,128)(2,1)} %bitcast.96, ...), custom_call_target="tpu_custom_call" | custom-call | flops 5898 | bytes 26542 | tf_op jit(solution)/shard_map/combine/pallas_call | solution.py:721
  168.2 16.3 %collective-permute-start.19 = (bf16[2,96,3840]{2,1,0:T(8,128)(2,1)}, bf16[2,96,3840]{2,1,0:T(8,128)(2,1)S(1)}, u32[]{:S(2)}, u32[]{:S(2)}) collective-permute-start(bf16[2,96,3840]{2,1,0:T(8,128)(2,1)} %get-tuple-element.225), channel_id=1, source_target_pairs={{0,8},{4,12},{8,0},{12,4},{16,24},{20,28},{24,16},{28,20},{1,9},{5... | collective-permute-start | bytes 4423688 | tf_op jit(solution)/shard_map/ppermute | solution.py:788
  189.2 17.5 %attend_back.4 = (f32[2,256,768]{2,1,0:T(8,128)}, bf16[2,256,768]{2,1,0:T(8,128)(2,1)}, f32[3,768,768]{2,1,0:T(8,128)}) custom-call(s32[3]{0:T(128)} %copy-done.34, bf16[256,768]{1,0:T(8,128)(2,1)} %copy-done.19, bf16[1024,768]{1,0:T(8,128)(2,1)} %copy-done.10, bf16[1024,768]{1,0:T(8,128)(2,1)} %copy-done.11, bf16[3,256,768]{2,1,0:T(8,128)(2,1)} %get-tuple-element.215.g_ref, ...), custom_call_target="tpu_custom_call" | custom-call | flops 12079595 | bytes 12000 | tf_op jit(solution)/shard_map/attend_back/pallas_call | solution.py:579
  206.7 8.4 %collective-permute-done.20 = bf16[2,384,768]{2,1,0:T(8,128)(2,1)S(1)} collective-permute-done((bf16[2,384,768]{2,1,0:T(8,128)(2,1)}, bf16[2,384,768]{2,1,0:T(8,128)(2,1)S(1)}, u32[]{:S(2)}, u32[]{:S(2)}) %collective-permute-start.20) | collective-permute-done | bytes 1179680 | tf_op jit(solution)/shard_map/ppermute | solution.py:788
  218.4 5.2 %combine.5 = (f32[1,96,3840]{2,1,0:T(8,128)}, bf16[1,96,3840]{2,1,0:T(8,128)(2,1)}, f32[1,384,768]{2,1,0:T(8,128)}, bf16[1,384,768]{2,1,0:T(8,128)(2,1)}) custom-call(s32[2]{0:T(128)} %pad_add_fusion.2.index, bf16[1,2,1,96,3840]{4,3,2,1,0:T(8,128)(2,1)} %bitcast.104, bf16[1,2,1,96,3840]{4,3,2,1,0:T(8,128)(2,1)} %bitcast.106, ...), custom_call_target="tpu_custom_call" | custom-call | flops 2949 | bytes 13271 | tf_op jit(solution)/shard_map/combine/pallas_call | solution.py:721
  225.4 3.7 %norm_one_back.3 = (f32[256,768]{1,0:T(8,128)}, bf16[256,768]{1,0:T(8,128)(2,1)}, f32[32,768]{1,0:T(8,128)}) custom-call(f32[2,256,768]{2,1,0:T(8,128)} %get-tuple-element.227.keep_ref, bf16[2,256,768]{2,1,0:T(8,128)(2,1)} %copy-done.47, bf16[256,768]{1,0:T(8,128)(2,1)} %copy-done.58, bf16[256,768]{1,0:T(8,128)(2,1)} %copy-done.16, ...), custom_call_target="tpu_custom_call" | custom-call | flops 7864 | bytes 6000 | tf_op jit(solution)/shard_map/norm_one_back/pallas_call | solution.py:623
  231.5 18.0 %attend_back.5 = (f32[2,256,768]{2,1,0:T(8,128)}, bf16[2,256,768]{2,1,0:T(8,128)(2,1)}, f32[4,96,1152]{2,1,0:T(8,128)}, bf16[4,96,1152]{2,1,0:T(8,128)(2,1)}, f3...) custom-call(s32[3]{0:T(128)} %copy-done.33, bf16[256,768]{1,0:T(8,128)(2,1)} %copy-done.18, ...), custom_call_target="tpu_custom_call" | custom-call | flops 12079595 | bytes 12000 | tf_op jit(solution)/shard_map/attend_back/pallas_call | solution.py:579
  252.3 3.7 %norm_one_back.4 = (f32[256,768]{1,0:T(8,128)}, bf16[256,768]{1,0:T(8,128)(2,1)}, f32[32,768]{1,0:T(8,128)}) custom-call(f32[2,256,768]{2,1,0:T(8,128)} %get-tuple-element.240.keep_ref, bf16[2,256,768]{2,1,0:T(8,128)(2,1)} %copy-done.46, bf16[256,768]{1,0:T(8,128)(2,1)} %copy-done.59, bf16[256,768]{1,0:T(8,128)(2,1)} %copy-done.15, ...), custom_call_target="tpu_custom_call" | custom-call | flops 7864 | bytes 6000 | tf_op jit(solution)/shard_map/norm_one_back/pallas_call | solution.py:623
  258.7 4.5 %combine.6 = (f32[2,96,1152]{2,1,0:T(8,128)}, bf16[2,96,1152]{2,1,0:T(8,128)(2,1)}, f32[2,96,1152]{2,1,0:T(8,128)}, bf16[2,96,1152]{2,1,0:T(8,128)(2,1)}) custom-call(s32[2]{0:T(128)} %pad_add_fusion.1.index, f32[2,2,1,96,1152]{4,3,2,1,0:T(8,128)} %bitcast.100, bf16[2,2,1,96,1152]{4,3,2,1,0:T(8,128)(2,1)} %bitcast.116, f32[2,2,1,96,1152]{4,3,2,1,0:T(8,128)} %bitcast.101, ...), custom_call_target="tpu_custom_call" | custom-call | flops 1769 | bytes 7962 | tf_op jit(solution)/shard_map/combine/pallas_call | solution.py:721
  263.2 3.6 %spread.2 = (f32[2,24,6912]{2,1,0:T(8,128)}, bf16[2,24,6912]{2,1,0:T(8,128)(2,1)}) custom-call(s32[1]{0:T(128)} %bitcast.8.place, f32[4,24,3840]{2,1,0:T(8,128)} %bitcast.126, bf16[4,24,3840]{2,1,0:T(8,128)(2,1)} %bitcast.130, f32[4,96,768]{2,1,0:T(8,128)} %bitcast.128, bf16[4,96,768]{2,1,0:T(8,128)(2,1)} %bitcast.131), custom_call_target="tpu_custom_call" | custom-call | flops 1327 | bytes 6635 | tf_op jit(solution)/shard_map/spread/pallas_call | solution.py:741
  268.7 7.9 %collective-permute-start.35 = (bf16[2,96,1152]{2,1,0:T(8,128)(2,1)}, bf16[2,96,1152]{2,1,0:T(8,128)(2,1)S(1)}, u32[]{:S(2)}, u32[]{:S(2)}) collective-permute-start(bf16[2,96,1152]{2,1,0:T(8,128)(2,1)} %get-tuple-element.274), channel_id=1, source_target_pairs={{0,8},{4,12},{8,0},{12,4},{16,24},{20,28},{24,16},{28,20},{1,9},{5... | collective-permute-start | bytes 1327112 | tf_op jit(solution)/shard_map/ppermute | solution.py:788
  277.6 3.6 %norm_one_back.5 = (f32[256,768]{1,0:T(8,128)}, bf16[256,768]{1,0:T(8,128)(2,1)}, f32[32,768]{1,0:T(8,128)}) custom-call(f32[2,256,768]{2,1,0:T(8,128)} %get-tuple-element.261.keep_ref, bf16[2,256,768]{2,1,0:T(8,128)(2,1)} %collective-permute-done.28.core_ref, bf16[256,768]{1,0:T(8,128)(2,1)} %copy-done.57, bf16[256,768]{1,0:T(8,128)(2,1)} %copy-done.14, ...), custom_call_target="tpu_custom_call" | custom-call | flops 7864 | bytes 6000 | tf_op jit(solution)/shard_map/norm_one_back/pallas_call | solution.py:623
  281.2 5.0 %collective-permute-done.35 = bf16[2,96,1152]{2,1,0:T(8,128)(2,1)S(1)} collective-permute-done((bf16[2,96,1152]{2,1,0:T(8,128)(2,1)}, bf16[2,96,1152]{2,1,0:T(8,128)(2,1)S(1)}, u32[]{:S(2)}, u32[]{:S(2)}) %collective-permute-start.35) | collective-permute-done | bytes 442400 | tf_op jit(solution)/shard_map/ppermute | solution.py:788
  288.2 3.7 %combine.7 = (f32[1,96,1152]{2,1,0:T(8,128)}, bf16[1,96,1152]{2,1,0:T(8,128)(2,1)}, f32[1,96,1152]{2,1,0:T(8,128)}, bf16[1,96,1152]{2,1,0:T(8,128)(2,1)}) custom-call(s32[2]{0:T(128)} %pad_add_fusion.2.index, f32[1,2,1,96,1152]{4,3,2,1,0:T(8,128)} %bitcast.112, bf16[1,2,1,96,1152]{4,3,2,1,0:T(8,128)(2,1)} %bitcast.122, f32[1,2,1,96,1152]{4,3,2,1,0:T(8,128)} %bitcast.113, ...), custom_call_target="tpu_custom_call" | custom-call | flops 884 | bytes 3981 | tf_op jit(solution)/shard_map/combine/pallas_call | solution.py:721
  293.8 4.3 %collective-permute-done.39 = bf16[1,96,1152]{2,1,0:T(8,128)(2,1)S(1)} collective-permute-done((bf16[1,96,1152]{2,1,0:T(8,128)(2,1)}, bf16[1,96,1152]{2,1,0:T(8,128)(2,1)S(1)}, u32[]{:S(2)}, u32[]{:S(2)}) %collective-permute-start.39) | collective-permute-done | bytes 221216 | tf_op jit(solution)/shard_map/ppermute | solution.py:788
  302.9 4.1 %collective-permute-start.46 = (bf16[24,6912]{1,0:T(8,128)(2,1)S(1)}, bf16[24,6912]{1,0:T(8,128)(2,1)S(1)}, u32[]{:S(2)}, u32[]{:S(2)}) collective-permute-start(bf16[24,6912]{1,0:T(8,128)(2,1)S(1)} %fusion.3), channel_id=1, source_target_pairs={{0,2},{1,3},{2,0},{3,1},{4,6},{5,7},{6,4},{7,5},{8,10},{9,11},{10,... | collective-permute-start | bytes 995336 | tf_op jit(solution)/shard_map/ppermute | solution.py:791
  314.3 7.2 %collective-permute-start.45 = (bf16[24,2304]{1,0:T(8,128)(2,1)S(1)}, bf16[24,2304]{1,0:T(8,128)(2,1)S(1)}, u32[]{:S(2)}, u32[]{:S(2)}) collective-permute-start(bf16[24,2304]{1,0:T(8,128)(2,1)S(1)} %fusion.11), channel_id=1, source_target_pairs={{0,2},{1,3},{2,0},{3,1},{4,6},{5,7},{6,4},{7,5},{8,10},{9,11},{10,... | collective-permute-start | bytes 331784 | tf_op jit(solution)/shard_map/ppermute | solution.py:791
  322.8 5.9 %put.1 = (bf16[3,256,768]{2,1,0:T(8,128)(2,1)}, f32[3,256,768]{2,1,0:T(8,128)}) custom-call(s32[4]{0:T(128)} %pad_add_fusion.order, bf16[3,256,768]{2,1,0:T(8,128)(2,1)} %get-tuple-element.213.refs_0_, bf16[3,256,768]{2,1,0:T(8,128)(2,1)} %collective-permute-done.22.refs_1_, f32[256,768]{1,0:T(8,128)} %get-tuple-element.239.refs_2_, ...), custom_call_target="tpu_custom_call" | custom-call | flops 1000 | bytes 10000 | tf_op jit(solution)/shard_map/put/pallas_call | solution.py:486
  328.7 5.2 %collective-permute-done.46.far_ref = bf16[24,6912]{1,0:T(8,128)(2,1)S(1)} collective-permute-done((bf16[24,6912]{1,0:T(8,128)(2,1)S(1)}, bf16[24,6912]{1,0:T(8,128)(2,1)S(1)}, u32[]{:S(2)}, u32[]{:S(2)}) %collective-permute-start.46) | collective-permute-done | bytes 331808 | tf_op jit(solution)/shard_map/ppermute | solution.py:791
  (292 shorter events, 84.9 us)
Async XLA Ops:
  6.6 9.9 %collective-permute-start.1 = (bf16[256,768]{1,0:T(8,128)(2,1)}, bf16[256,768]{1,0:T(8,128)(2,1)}, u32[]{:S(2)}, u32[]{:S(2)}) collective-permute-start(bf16[256,768]{1,0:T(8,128)(2,1)} %get-tuple-element.167), channel_id=1, source_target_pairs={{2,4},{3,5},{4,2},{5,3},{10,12},{11,13},{12,10},{13,11},{18,20},{1... | collective-permute-start | bytes 1179656 | tf_op jit(solution)/shard_map/ppermute | solution.py:806
  17.6 11.7 %collective-permute-start.2 = (bf16[256,768]{1,0:T(8,128)(2,1)S(1)}, bf16[256,768]{1,0:T(8,128)(2,1)S(1)}, u32[]{:S(2)}, u32[]{:S(2)}) collective-permute-start(bf16[256,768]{1,0:T(8,128)(2,1)S(1)} %broadcast_select_fusion.2.a_ref.tok_ref), channel_id=1, source_target_pairs={{0,1},{1,0},{2,3},{3,2},{4,5},{5,4},{6,7},{7,6},{8,9},{9,8},{10,11... | collective-permute-start | bytes 1179656 | tf_op jit(solution)/shard_map/ppermute | solution.py:791
  20.3 10.2 %collective-permute-start.5 = (bf16[256,768]{1,0:T(8,128)(2,1)}, bf16[256,768]{1,0:T(8,128)(2,1)S(1)}, u32[]{:S(2)}, u32[]{:S(2)}) collective-permute-start(bf16[256,768]{1,0:T(8,128)(2,1)} %copy-done.28), channel_id=1, source_target_pairs={{2,4},{3,5},{4,2},{5,3},{10,12},{11,13},{12,10},{13,11},{18,20},{1... | collective-permute-start | bytes 1179656 | tf_op jit(solution)/shard_map/ppermute | solution.py:806
  20.9 13.0 %collective-permute-start.3 = (bf16[256,768]{1,0:T(8,128)(2,1)S(1)}, bf16[256,768]{1,0:T(8,128)(2,1)S(1)}, u32[]{:S(2)}, u32[]{:S(2)}) collective-permute-start(bf16[256,768]{1,0:T(8,128)(2,1)S(1)} %broadcast_select_fusion.2.a_ref.tok_ref), channel_id=1, source_target_pairs={{0,4},{4,0},{8,12},{12,8},{16,20},{20,16},{24,28},{28,24},{1,5},{5... | collective-permute-start | bytes 1179656 | tf_op jit(solution)/shard_map/ppermute | solution.py:788
  31.6 15.7 %collective-permute-start.6 = (bf16[256,768]{1,0:T(8,128)(2,1)S(1)}, bf16[256,768]{1,0:T(8,128)(2,1)S(1)}, u32[]{:S(2)}, u32[]{:S(2)}) collective-permute-start(bf16[256,768]{1,0:T(8,128)(2,1)S(1)} %broadcast_select_fusion.1.a_ref.tok_ref), channel_id=1, source_target_pairs={{0,1},{1,0},{2,3},{3,2},{4,5},{5,4},{6,7},{7,6},{8,9},{9,8},{10,11... | collective-permute-start | bytes 1179656 | tf_op jit(solution)/shard_map/ppermute | solution.py:791
  33.2 24.3 %collective-permute-start.9 = (bf16[256,768]{1,0:T(8,128)(2,1)}, bf16[256,768]{1,0:T(8,128)(2,1)S(1)}, u32[]{:S(2)}, u32[]{:S(2)}) collective-permute-start(bf16[256,768]{1,0:T(8,128)(2,1)} %copy-done.26), channel_id=1, source_target_pairs={{2,4},{3,5},{4,2},{5,3},{10,12},{11,13},{12,10},{13,11},{18,20},{1... | collective-permute-start | bytes 1179656 | tf_op jit(solution)/shard_map/ppermute | solution.py:806
  47.3 12.6 %collective-permute-start.7 = (bf16[256,768]{1,0:T(8,128)(2,1)S(1)}, bf16[256,768]{1,0:T(8,128)(2,1)S(1)}, u32[]{:S(2)}, u32[]{:S(2)}) collective-permute-start(bf16[256,768]{1,0:T(8,128)(2,1)S(1)} %broadcast_select_fusion.1.a_ref.tok_ref), channel_id=1, source_target_pairs={{0,4},{4,0},{8,12},{12,8},{16,20},{20,16},{24,28},{28,24},{1,5},{5... | collective-permute-start | bytes 1179656 | tf_op jit(solution)/shard_map/ppermute | solution.py:788
  57.6 14.7 %collective-permute-start.10 = (bf16[256,768]{1,0:T(8,128)(2,1)S(1)}, bf16[256,768]{1,0:T(8,128)(2,1)S(1)}, u32[]{:S(2)}, u32[]{:S(2)}) collective-permute-start(bf16[256,768]{1,0:T(8,128)(2,1)S(1)} %broadcast_select_fusion.a_ref.tok_ref), channel_id=1, source_target_pairs={{0,1},{1,0},{2,3},{3,2},{4,5},{5,4},{6,7},{7,6},{8,9},{9,8},{10,11... | collective-permute-start | bytes 1179656 | tf_op jit(solution)/shard_map/ppermute | solution.py:791
  58.4 22.1 %collective-permute-start.13 = (bf16[256,768]{1,0:T(8,128)(2,1)S(1)}, bf16[256,768]{1,0:T(8,128)(2,1)S(1)}, u32[]{:S(2)}, u32[]{:S(2)}) collective-permute-start(bf16[256,768]{1,0:T(8,128)(2,1)S(1)} %get-tuple-element.196), channel_id=1, source_target_pairs={{2,4},{3,5},{4,2},{5,3},{10,12},{11,13},{12,10},{13,11},{18,20},{1... | collective-permute-start | bytes 1179656 | tf_op jit(solution)/shard_map/ppermute | solution.py:806
  59.1 21.4 %collective-permute-start.14 = (bf16[256,768]{1,0:T(8,128)(2,1)S(1)}, bf16[256,768]{1,0:T(8,128)(2,1)S(1)}, u32[]{:S(2)}, u32[]{:S(2)}) collective-permute-start(bf16[256,768]{1,0:T(8,128)(2,1)S(1)} %get-tuple-element.198), channel_id=1, source_target_pairs={{2,4},{3,5},{4,2},{5,3},{10,12},{11,13},{12,10},{13,11},{18,20},{1... | collective-permute-start | bytes 1179656 | tf_op jit(solution)/shard_map/ppermute | solution.py:806
  135.4 22.8 %collective-permute-start.16 = (bf16[4,96,3840]{2,1,0:T(8,128)(2,1)}, bf16[4,96,3840]{2,1,0:T(8,128)(2,1)S(1)}, u32[]{:S(2)}, u32[]{:S(2)}) collective-permute-start(bf16[4,96,3840]{2,1,0:T(8,128)(2,1)} %get-tuple-element.220), channel_id=1, source_target_pairs={{0,4},{4,0},{8,12},{12,8},{16,20},{20,16},{24,28},{28,24},{1,5},{5... | collective-permute-start | bytes 8847368 | tf_op jit(solution)/shard_map/ppermute | solution.py:788
  142.2 15.9 %collective-permute-start.17 = (bf16[4,384,768]{2,1,0:T(8,128)(2,1)}, bf16[4,384,768]{2,1,0:T(8,128)(2,1)}, u32[]{:S(2)}, u32[]{:S(2)}) collective-permute-start(bf16[4,384,768]{2,1,0:T(8,128)(2,1)} %get-tuple-element.221), channel_id=1, source_target_pairs={{0,4},{4,0},{8,12},{12,8},{16,20},{20,16},{24,28},{28,24},{1,5},{5... | collective-permute-start | bytes 7077896 | tf_op jit(solution)/shard_map/ppermute | solution.py:788
  168.2 49.1 %collective-permute-start.19 = (bf16[2,96,3840]{2,1,0:T(8,128)(2,1)}, bf16[2,96,3840]{2,1,0:T(8,128)(2,1)S(1)}, u32[]{:S(2)}, u32[]{:S(2)}) collective-permute-start(bf16[2,96,3840]{2,1,0:T(8,128)(2,1)} %get-tuple-element.225), channel_id=1, source_target_pairs={{0,8},{4,12},{8,0},{12,4},{16,24},{20,28},{24,16},{28,20},{1,9},{5... | collective-permute-start | bytes 4423688 | tf_op jit(solution)/shard_map/ppermute | solution.py:788
  184.5 22.2 %collective-permute-start.22 = (bf16[3,256,768]{2,1,0:T(8,128)(2,1)}, bf16[3,256,768]{2,1,0:T(8,128)(2,1)}, u32[]{:S(2)}, u32[]{:S(2)}) collective-permute-start(bf16[3,256,768]{2,1,0:T(8,128)(2,1)} %get-tuple-element.213.refs_0_), channel_id=1, source_target_pairs={{2,4},{3,5},{4,2},{5,3},{10,12},{11,13},{12,10},{13,11},{18,20},{1... | collective-permute-start | bytes 3538952 | tf_op jit(solution)/shard_map/ppermute | solution.py:806
  186.2 28.8 %collective-permute-start.20 = (bf16[2,384,768]{2,1,0:T(8,128)(2,1)}, bf16[2,384,768]{2,1,0:T(8,128)(2,1)S(1)}, u32[]{:S(2)}, u32[]{:S(2)}) collective-permute-start(bf16[2,384,768]{2,1,0:T(8,128)(2,1)} %get-tuple-element.226), channel_id=1, source_target_pairs={{0,16},{4,20},{8,24},{12,28},{16,0},{20,4},{24,8},{28,12},{1,17},{... | collective-permute-start | bytes 3538952 | tf_op jit(solution)/shard_map/ppermute | solution.py:788
  189.1 26.0 %collective-permute-start.21 = (bf16[256,768]{1,0:T(8,128)(2,1)S(1)}, bf16[256,768]{1,0:T(8,128)(2,1)S(1)}, u32[]{:S(2)}, u32[]{:S(2)}) collective-permute-start(bf16[256,768]{1,0:T(8,128)(2,1)S(1)} %fusion), channel_id=1, source_target_pairs={{0,1},{1,0},{2,3},{3,2},{4,5},{5,4},{6,7},{7,6},{8,9},{9,8},{10,11... | collective-permute-start | bytes 1179656 | tf_op jit(solution)/shard_map/ppermute | solution.py:791
  217.3 13.2 %collective-permute-start.23 = (bf16[2,256,768]{2,1,0:T(8,128)(2,1)}, bf16[2,256,768]{2,1,0:T(8,128)(2,1)S(1)}, u32[]{:S(2)}, u32[]{:S(2)}) collective-permute-start(bf16[2,256,768]{2,1,0:T(8,128)(2,1)} %get-tuple-element.241), channel_id=1, source_target_pairs={{0,4},{4,0},{8,12},{12,8},{16,20},{20,16},{24,28},{28,24},{1,5},{5... | collective-permute-start | bytes 2359304 | tf_op jit(solution)/shard_map/ppermute | solution.py:788
  223.6 25.9 %collective-permute-start.24 = (bf16[1,96,3840]{2,1,0:T(8,128)(2,1)}, bf16[1,96,3840]{2,1,0:T(8,128)(2,1)S(1)}, u32[]{:S(2)}, u32[]{:S(2)}) collective-permute-start(bf16[1,96,3840]{2,1,0:T(8,128)(2,1)} %get-tuple-element.246), channel_id=1, source_target_pairs={{0,16},{4,20},{8,24},{12,28},{16,0},{20,4},{24,8},{28,12},{1,17},{... | collective-permute-start | bytes 2211848 | tf_op jit(solution)/shard_map/ppermute | solution.py:788
  223.6 25.9 %collective-permute-start.25 = (bf16[1,384,768]{2,1,0:T(8,128)(2,1)}, bf16[1,384,768]{2,1,0:T(8,128)(2,1)S(1)}, u32[]{:S(2)}, u32[]{:S(2)}) collective-permute-start(bf16[1,384,768]{2,1,0:T(8,128)(2,1)} %get-tuple-element.247), channel_id=1, source_target_pairs={{0,8},{4,12},{8,0},{12,4},{16,24},{20,28},{24,16},{28,20},{1,9},{5... | collective-permute-start | bytes 1769480 | tf_op jit(solution)/shard_map/ppermute | solution.py:788
  229.1 20.4 %collective-permute-start.27 = (bf16[256,768]{1,0:T(8,128)(2,1)}, bf16[256,768]{1,0:T(8,128)(2,1)}, u32[]{:S(2)}, u32[]{:S(2)}) collective-permute-start(bf16[256,768]{1,0:T(8,128)(2,1)} %get-tuple-element.248), channel_id=1, source_target_pairs={{2,4},{3,5},{4,2},{5,3},{10,12},{11,13},{12,10},{13,11},{18,20},{1... | collective-permute-start | bytes 1179656 | tf_op jit(solution)/shard_map/ppermute | solution.py:806
  231.5 18.1 %collective-permute-start.26 = (bf16[256,768]{1,0:T(8,128)(2,1)}, bf16[256,768]{1,0:T(8,128)(2,1)S(1)}, u32[]{:S(2)}, u32[]{:S(2)}) collective-permute-start(bf16[256,768]{1,0:T(8,128)(2,1)} %fusion.1), channel_id=1, source_target_pairs={{0,1},{1,0},{2,3},{3,2},{4,5},{5,4},{6,7},{7,6},{8,9},{9,8},{10,11... | collective-permute-start | bytes 1179656 | tf_op jit(solution)/shard_map/ppermute | solution.py:791
  257.0 11.1 %collective-permute-start.29 = (bf16[256,768]{1,0:T(8,128)(2,1)S(1)}, bf16[256,768]{1,0:T(8,128)(2,1)S(1)}, u32[]{:S(2)}, u32[]{:S(2)}) collective-permute-start(bf16[256,768]{1,0:T(8,128)(2,1)S(1)} %fusion.2), channel_id=1, source_target_pairs={{0,1},{1,0},{2,3},{3,2},{4,5},{5,4},{6,7},{7,6},{8,9},{9,8},{10,11... | collective-permute-start | bytes 1179656 | tf_op jit(solution)/shard_map/ppermute | solution.py:791
  268.1 25.5 %collective-permute-start.32 = (bf16[2,24,6912]{2,1,0:T(8,128)(2,1)}, bf16[2,24,6912]{2,1,0:T(8,128)(2,1)S(1)}, u32[]{:S(2)}, u32[]{:S(2)}) collective-permute-start(bf16[2,24,6912]{2,1,0:T(8,128)(2,1)} %get-tuple-element.284), channel_id=1, source_target_pairs={{0,1},{1,0},{2,3},{3,2},{4,5},{5,4},{6,7},{7,6},{8,9},{9,8},{10,11... | collective-permute-start | bytes 1990664 | tf_op jit(solution)/shard_map/ppermute | solution.py:917
  268.7 17.4 %collective-permute-start.35 = (bf16[2,96,1152]{2,1,0:T(8,128)(2,1)}, bf16[2,96,1152]{2,1,0:T(8,128)(2,1)S(1)}, u32[]{:S(2)}, u32[]{:S(2)}) collective-permute-start(bf16[2,96,1152]{2,1,0:T(8,128)(2,1)} %get-tuple-element.274), channel_id=1, source_target_pairs={{0,8},{4,12},{8,0},{12,4},{16,24},{20,28},{24,16},{28,20},{1,9},{5... | collective-permute-start | bytes 1327112 | tf_op jit(solution)/shard_map/ppermute | solution.py:788
  276.6 10.8 %collective-permute-start.36 = (bf16[2,96,1152]{2,1,0:T(8,128)(2,1)S(1)}, bf16[2,96,1152]{2,1,0:T(8,128)(2,1)S(1)}, u32[]{:S(2)}, u32[]{:S(2)}) collective-permute-start(bf16[2,96,1152]{2,1,0:T(8,128)(2,1)S(1)} %copy-done.69), channel_id=1, source_target_pairs={{0,16},{4,20},{8,24},{12,28},{16,0},{20,4},{24,8},{28,12},{1,17},{... | collective-permute-start | bytes 1327112 | tf_op jit(solution)/shard_map/ppermute | solution.py:788
  276.6 17.0 %collective-permute-start.33 = (bf16[256,768]{1,0:T(8,128)(2,1)}, bf16[256,768]{1,0:T(8,128)(2,1)S(1)}, u32[]{:S(2)}, u32[]{:S(2)}) collective-permute-start(bf16[256,768]{1,0:T(8,128)(2,1)} %get-tuple-element.285), channel_id=1, source_target_pairs={{2,4},{3,5},{4,2},{5,3},{10,12},{11,13},{12,10},{13,11},{18,20},{1... | collective-permute-start | bytes 1179656 | tf_op jit(solution)/shard_map/ppermute | solution.py:806
  281.2 11.4 %collective-permute-start.34 = (f32[32,768]{1,0:T(8,128)}, f32[32,768]{1,0:T(8,128)S(1)}, u32[]{:S(2)}, u32[]{:S(2)}) collective-permute-start(f32[32,768]{1,0:T(8,128)} %get-tuple-element.286), channel_id=1, source_target_pairs={{0,4},{4,0},{8,12},{12,8},{16,20},{20,16},{24,28},{28,24},{1,5},{5... | collective-permute-start | bytes 294920 | tf_op jit(solution)/shard_map/ppermute | solution.py:788
  292.6 8.4 %collective-permute-start.38 = (f32[32,768]{1,0:T(8,128)S(1)}, f32[32,768]{1,0:T(8,128)S(1)}, u32[]{:S(2)}, u32[]{:S(2)}) collective-permute-start(f32[32,768]{1,0:T(8,128)S(1)} %add.59), channel_id=1, source_target_pairs={{0,1},{1,0},{2,3},{3,2},{4,5},{5,4},{6,7},{7,6},{8,9},{9,8},{10,11... | collective-permute-start | bytes 294920 | tf_op jit(solution)/shard_map/ppermute | solution.py:791
  301.2 20.5 %collective-permute-start.37 = (bf16[256,768]{1,0:T(8,128)(2,1)}, bf16[256,768]{1,0:T(8,128)(2,1)S(1)}, u32[]{:S(2)}, u32[]{:S(2)}) collective-permute-start(bf16[256,768]{1,0:T(8,128)(2,1)} %get-tuple-element.288), channel_id=1, source_target_pairs={{2,4},{3,5},{4,2},{5,3},{10,12},{11,13},{12,10},{13,11},{18,20},{1... | collective-permute-start | bytes 1179656 | tf_op jit(solution)/shard_map/ppermute | solution.py:806
  302.9 31.0 %collective-permute-start.46 = (bf16[24,6912]{1,0:T(8,128)(2,1)S(1)}, bf16[24,6912]{1,0:T(8,128)(2,1)S(1)}, u32[]{:S(2)}, u32[]{:S(2)}) collective-permute-start(bf16[24,6912]{1,0:T(8,128)(2,1)S(1)} %fusion.3), channel_id=1, source_target_pairs={{0,2},{1,3},{2,0},{3,1},{4,6},{5,7},{6,4},{7,5},{8,10},{9,11},{10,... | collective-permute-start | bytes 995336 | tf_op jit(solution)/shard_map/ppermute | solution.py:791
  311.8 9.6 %collective-permute-start.44 = (bf16[4,26,768]{2,1,0:T(8,128)(2,1)S(1)}, bf16[4,26,768]{2,1,0:T(8,128)(2,1)S(1)}, u32[]{:S(2)}, u32[]{:S(2)}) collective-permute-start(bf16[4,26,768]{2,1,0:T(8,128)(2,1)S(1)} %pad_maximum_fusion.3), channel_id=1, source_target_pairs={{0,16},{4,20},{8,24},{12,28},{16,0},{20,4},{24,8},{28,12},{1,17},{... | collective-permute-start | bytes 479240 | tf_op jit(solution)/shard_map/ppermute | solution.py:788
  314.3 23.7 %collective-permute-start.45 = (bf16[24,2304]{1,0:T(8,128)(2,1)S(1)}, bf16[24,2304]{1,0:T(8,128)(2,1)S(1)}, u32[]{:S(2)}, u32[]{:S(2)}) collective-permute-start(bf16[24,2304]{1,0:T(8,128)(2,1)S(1)} %fusion.11), channel_id=1, source_target_pairs={{0,2},{1,3},{2,0},{3,1},{4,6},{5,7},{6,4},{7,5},{8,10},{9,11},{10,... | collective-permute-start | bytes 331784 | tf_op jit(solution)/shard_map/ppermute | solution.py:791
  (85 other events, 799.3 us)
where the time goes:
time: 348 us; the launch traced here: 343 us
  Pallas kernels  173 us (50%)
  starting transfers between devices  91.3 us (26%)
  waiting for transfers between devices  32.5 us (9%)
  local copies, waits for them, and re-layouts  25.1 us (7%)
  other arithmetic  14.5 us (4%)
  matrix products  4.78 us (1%)
    ppermute x25, starting transfers between devices, dp_swap(): lax.ppermute(value, 'dp', [(i, i ^ 1 << bit) for i in range(dp_size)])  62.6 us
    pallas_call x3, Pallas kernels, attend_back(): pl.pallas_call(functools.partial(attend_back_kernel, more, last), grid_sp...  51.3 us
    pallas_call x1, Pallas kernels, feed_forward(): pl.pallas_call(mlp_kernel, grid_spec=pltpu.PrefetchScalarGridSpec(num_sca...  41.6 us
    ppermute x25, waiting for transfers between devices, dp_swap(): lax.ppermute(value, 'dp', [(i, i ^ 1 << bit) for i in range(dp_size)])  24.7 us
    pallas_call x4, Pallas kernels, combine(): pl.pallas_call(combine_kernel, grid_spec=pltpu.PrefetchScalarGridSpec(num...  21.8 us
    unnamed x144, local copies, waits for them, and re-layouts  18.9 us
    ppermute x10, starting transfers between devices, seq_swap(): lax.ppermute(value, 'seq', [(i, i ^ 1 << bit) for i in range(seq_size)])  17.2 us
    pallas_call x3, Pallas kernels, attend(): pl.pallas_call(attend_kernel, grid_spec=pltpu.PrefetchScalarGridSpec(num_...  15.5 us
  transfers between devices with their start and end apart: 47, of which 11 were waited for; matrix products, arithmetic and copies ran while one was open for 6% of the time, Pallas kernels for 33%

commit v1 on v0

--- a/solution.py
+++ b/solution.py
@@ -64,7 +64,7 @@
 
 def arrange_kernel(lengths, tok_ref, cond_ref, *refs):
     parts = tok_ref.shape[0]
-    tok_refs, both_ref, order_ref = refs[:parts], refs[parts], refs[parts + 1]
+    first_ref, rest_ref, both_ref, order_ref = refs
     rank = []
     for s in range(parts):
         ahead = jnp.int32(0)
@@ -79,7 +79,10 @@
         at = jnp.int32(0)
         for k in range(1, parts):
             at = jnp.where(rank[k] == r, k, at)
-        tok_refs[r][...] = tok_ref[at]
+        if r == 0:
+            first_ref[0] = tok_ref[at]
+        else:
+            rest_ref[r - 1] = tok_ref[at]
         width = cond_ref.shape[1]
         both_ref[r : r + 1, :width] = cond_ref[pl.ds(at, 1), :]
         both_ref[r : r + 1, width:] = jnp.full((1, LANES), lengths[at]).astype(F32)
@@ -87,9 +90,9 @@
         order_ref[parts + r] = rank[r]
 
 
-def arrange_pulls_kernel(order, pull_ref, *refs):
-    for r, ref in enumerate(refs):
-        ref[...] = pull_ref[order[r]]
+def arrange_pulls_kernel(order, pull_ref, out_ref):
+    for r in range(pull_ref.shape[0]):
+        out_ref[r] = pull_ref[order[r]]
 
 
 def put_kernel(order, *refs):
@@ -111,63 +114,81 @@
             grad_ref[0] = moves[s][...].astype(F32)
 
 
-def prep_kernel(
+def front_kernel(
     place, a_ref, b_ref, c_ref, d_ref, mod_ref, gain_ref, w_ref, cos_ref, sin_ref,
-    actt_ref, q_ref, k_ref, v_ref,
+    actt_ref, q_ref, k_ref, v_ref, mix_ref, lse_ref, queries, keys, values,
 ):
-    step = pl.program_id(0)
+    step, length = pl.program_id(1), place[1 + pl.program_id(0)]
     rows, width = a_ref.shape
-    source = jnp.where(
-        step < 2,
-        jnp.where(step == 0, a_ref[...], b_ref[...]),
-        jnp.where(step == 2, c_ref[...], d_ref[...]),
-    ).astype(F32)
-    normed, _ = normalize(source)
-    act = (normed * gain_ref[...] * (1.0 + mod_ref[0, 1:2, :]) + mod_ref[0, 0:1, :]).astype(BF)
-    actt_ref[...] = act.T
-    cosine, sine = cos_ref[...], sin_ref[...]
-
-    def turned(start, out_ref, factor):
-        for at in range(0, width, BLOCK):
-            both = nn(act, w_ref[:, start + at : start + at + BLOCK])
-            for lane in range(0, BLOCK, LANES):
-                part = both[:, lane : lane + LANES]
-                out_ref[:, at + lane : at + lane + LANES] = (
-                    part * cosine + swap_halves(part) * sine
-                ).astype(BF) * factor
-
-    @pl.when((place[0] ^ step) * rows < place[1])
+    groups = width // BLOCK
+    chunk = place[0] ^ jnp.minimum(step, 3)
+    here = pl.ds(pl.multiple_of(chunk * rows, rows), rows)
+
+    def turned(act, start, group):
+        at = start + group * BLOCK
+        both = nn(act, w_ref[:, at : at + BLOCK])
+        cosine, sine = cos_ref[...], sin_ref[...]
+        parts = []
+        for lane in range(0, BLOCK, LANES):
+            part = both[:, lane : lane + LANES]
+            parts.append((part * cosine + swap_halves(part) * sine).astype(BF))
+        return jnp.concatenate(parts, axis=1)
+
+    @pl.when(step < 4)
     def _():
-        turned(width, k_ref, BF(1.0))
-        v_ref[...] = nn(act, w_ref[:, 2 * width :]).astype(BF)
-
-    @pl.when(step == 0)
-    def _():
-        turned(0, q_ref, BF(HD**-0.5))
-
-
-def attend_kernel(place, q_ref, k_ref, v_ref, mix_ref, lse_ref):
+        source = jnp.where(
+            step < 2,
+            jnp.where(step == 0, a_ref[...], b_ref[...]),
+            jnp.where(step == 2, c_ref[...], d_ref[...]),
+        ).astype(F32)
+        normed, _ = normalize(source)
+        act = (normed * gain_ref[...] * (1.0 + mod_ref[0, 1:2, :]) + mod_ref[0, 0:1, :]).astype(BF)
+        actt_ref[...] = act.T
+
+        @pl.when(chunk * rows < length)
+        def _():
+            for group in range(groups):
+                lanes = slice(group * BLOCK, (group + 1) * BLOCK)
+                key = turned(act, width, group)
+                k_ref[:, lanes] = key
+                keys[group, here, :] = key
+                at = 2 * width + group * BLOCK
+                value = nn(act, w_ref[:, at : at + BLOCK]).astype(BF)
+                v_ref[:, lanes] = value
+                values[group, here, :] = value
+
+        @pl.when(step == 0)
+        def _():
+            for group in range(groups):
+                query = turned(act, 0, group) * BF(HD**-0.5)
+                q_ref[:, group * BLOCK : (group + 1) * BLOCK] = query
+                queries[group] = query
+
     masks = head_masks()
     lane = lax.broadcasted_iota(jnp.int32, (1, BLOCK), 1)
     narrow = lax.broadcasted_iota(jnp.int32, (1, LANES), 1)
 
     def work(span):
-        queries, keys, values = q_ref[...], k_ref[:span, :], v_ref[:span, :]
-        mixed = jnp.zeros(q_ref.shape, F32)
-        logs = jnp.zeros((q_ref.shape[0], LANES), F32)
+        group = step - 4
+        query = queries[group]
+        stacked = jnp.concatenate([query * masks[h] for h in range(PACK)], axis=0)
+        scores = nt(stacked, keys[group, :span, :])
+        top = jnp.max(scores, axis=-1, keepdims=True)
+        raised = jnp.exp(scores - top)
+        total = jnp.sum(raised, axis=-1, keepdims=True)
+        probs = (raised * (1.0 / total)).astype(BF)
+        level = top + jnp.log(total)
+        logs = jnp.zeros((rows, LANES), F32)
+        result = jnp.zeros((rows, BLOCK), F32)
         for head in range(PACK):
-            scores = nt(queries * masks[head], keys)
-            top = jnp.max(scores, axis=-1, keepdims=True)
-            raised = jnp.exp(scores - top)
-            total = jnp.sum(raised, axis=-1, keepdims=True)
-            probs = (raised * (1.0 / total)).astype(BF)
-            mixed = jnp.where(lane // HD == head, nn(probs, values), mixed)
-            logs = jnp.where(narrow == head, top + jnp.log(total), logs)
-        mix_ref[...] = mixed.astype(BF)
+            part = slice(head * rows, (head + 1) * rows)
+            result = jnp.where(lane // HD == head, nn(probs[part], values[group, :span, :]), result)
+            logs = jnp.where(narrow == head, level[part], logs)
+        mix_ref[...] = result.astype(BF)
         lse_ref[0] = logs.T[:8, :]
 
     for span in SPANS:
-        pl.when(place[1] == span)(functools.partial(work, span))
+        pl.when((step >= 4) & (length == span))(functools.partial(work, span))
 
 
 def attend_back_kernel(
@@ -332,7 +353,7 @@
 
 
 def mlp_kernel(
-    core, mix0_ref, mix1_ref, mix2_ref, tok_ref, cot_ref, mod_ref, gain_ref, wout_ref, bdown_ref,
+    core, mix0_ref, mix1_ref, mix2_ref, tok0_ref, tok1_ref, tok2_ref, cot_ref, mod_ref, gain_ref, wout_ref, bdown_ref,
     wup_ref, bup_ref, wdown_ref,
     out_ref, gres_ref, gmix_ref, sums_ref,
     keepup_ref, sendup_ref, keepdown_ref, senddown_ref,
@@ -340,8 +361,8 @@
 ):
     step = pl.program_id(0)
     tiles = pl.num_programs(0) // 2
-    parts, rows, _ = tok_ref.shape
-    mixes = (mix0_ref, mix1_ref, mix2_ref)
+    parts, rows, _ = cot_ref.shape
+    mixes, tokens = (mix0_ref, mix1_ref, mix2_ref), (tok0_ref, tok1_ref, tok2_ref)
 
     def span(s):
         return slice(s * rows, (s + 1) * rows)
@@ -354,7 +375,7 @@
         sums_ref[...] = jnp.zeros_like(sums_ref)
         for s in range(parts):
             one = nn(mixes[s][...], wout_ref[...])
-            res = tok_ref[s].astype(F32) + mod(s, 2) * one
+            res = tokens[s][...].astype(F32) + mod(s, 2) * one
             branch[span(s), :] = one
             resid[span(s), :] = res
             normed, _ = normalize(res)
@@ -444,7 +465,7 @@
 
 def arrange(lengths, tokens, cond):
     parts, rows, width = tokens.shape
-    shapes = [jax.ShapeDtypeStruct((rows, width), BF)] * parts
+    shapes = [jax.ShapeDtypeStruct((n, rows, width), BF) for n in (1, parts - 1)]
     shapes.append(jax.ShapeDtypeStruct((8, cond.shape[1] + LANES), F32))
     return pl.pallas_call(
         arrange_kernel,
@@ -462,17 +483,15 @@
 
 
 def arrange_pulls(order, pulls):
-    parts, rows, width = pulls.shape
-    shapes = [jax.ShapeDtypeStruct((rows, width), BF)] * parts
     return pl.pallas_call(
         arrange_pulls_kernel,
         grid_spec=pltpu.PrefetchScalarGridSpec(
             num_scalar_prefetch=1,
             grid=(1,),
             in_specs=[whole(pulls)],
-            out_specs=[whole(v) for v in shapes],
+            out_specs=whole(pulls),
         ),
-        out_shape=shapes,
+        out_shape=jax.ShapeDtypeStruct(pulls.shape, BF),
         compiler_params=limits(32),
         cost_estimate=cost(1e6, 3e6),
         name="arrange_pulls",
@@ -501,69 +520,56 @@
     )(order, value, moved, *grads, *moves)
 
 
-def prepare(place, pieces, mod, s, gain, w_qkv, cosine, sine):
-    rows, width = pieces[0].shape
-    slots = 4 * rows
-    table = pl.BlockSpec((rows, LANES), lambda i, p: (p[0] ^ i, 0))
-    piece = pl.BlockSpec((rows, width), lambda i, p: (p[0] ^ i, 0))
+def front(place, pieces, mod, first, gain, w_qkv, cosine, sine):
+    count, rows, width = pieces[0].shape
+    slots, groups = 4 * rows, width // BLOCK
+    chunk = lambda i, p: p[0] ^ jnp.minimum(i, 3)
+    group = lambda i: jnp.maximum(i - 4, 0)
+    table = pl.BlockSpec((rows, LANES), lambda s, i, p: (chunk(i, p), 0))
+    piece = pl.BlockSpec((None, rows, width), lambda s, i, p: (s, chunk(i, p), 0))
     return pl.pallas_call(
-        prep_kernel,
+        front_kernel,
         grid_spec=pltpu.PrefetchScalarGridSpec(
             num_scalar_prefetch=1,
-            grid=(4,),
-            in_specs=[whole(a) for a in pieces]
-            + [pl.BlockSpec((1,) + mod.shape[1:], lambda i, p: (s, 0, 0))]
+            grid=(count, 4 + groups),
+            in_specs=[pl.BlockSpec((None, rows, width), lambda s, i, p: (s, 0, 0))] * 4
+            + [pl.BlockSpec((1,) + mod.shape[1:], lambda s, i, p: (first + s, 0, 0))]
             + [whole(gain), whole(w_qkv), table, table],
             out_specs=[
-                pl.BlockSpec((width, rows), lambda i, p: (0, p[0] ^ i)),
-                pl.BlockSpec((rows, width), lambda i, p: (0, 0)),
+                pl.BlockSpec((None, width, rows), lambda s, i, p: (s, 0, chunk(i, p))),
+                pl.BlockSpec((None, rows, width), lambda s, i, p: (s, 0, 0)),
                 piece, piece,
+                pl.BlockSpec((None, rows, BLOCK), lambda s, i, p: (s, 0, group(i))),
+                pl.BlockSpec((None, 1, 8, rows), lambda s, i, p: (s, group(i), 0, 0)),
+            ],
+            scratch_shapes=[
+                pltpu.VMEM((groups, rows, BLOCK), BF),
+                pltpu.VMEM((groups, slots, BLOCK), BF),
+                pltpu.VMEM((groups, slots, BLOCK), BF),
             ],
         ),
         out_shape=[
-            jax.ShapeDtypeStruct((width, slots), BF),
-            jax.ShapeDtypeStruct((rows, width), BF),
-            jax.ShapeDtypeStruct((slots, width), BF),
-            jax.ShapeDtypeStruct((slots, width), BF),
+            jax.ShapeDtypeStruct((count, width, slots), BF),
+            jax.ShapeDtypeStruct((count, rows, width), BF),
+            jax.ShapeDtypeStruct((count, slots, width), BF),
+            jax.ShapeDtypeStruct((count, slots, width), BF),
+            jax.ShapeDtypeStruct((count, rows, width), BF),
+            jax.ShapeDtypeStruct((count, groups, 8, rows), F32),
         ],
-        compiler_params=limits(32),
-        cost_estimate=cost(2 * slots * width * width * 2.25, 10e6),
-        name="prepare",
+        compiler_params=limits(40),
+        cost_estimate=cost(2 * count * slots * width * width * 3, 15e6 * count),
+        name="front",
     )(place, *pieces, mod, gain, w_qkv, cosine, sine)
 
 
-def attend(place, queries, keys, values):
-    rows, width = queries.shape
-    slots = keys.shape[0]
+def attend_back(
+    place, at, queries, keys, values, grads, s, logs, cosine, sine, w_qkv, act_t, before, last, dp_size
+):
+    _, rows, width = queries.shape
+    slots = keys.shape[1]
     groups = width // BLOCK
-    own = pl.BlockSpec((rows, BLOCK), lambda j, p: (0, j))
-    full = pl.BlockSpec((slots, BLOCK), lambda j, p: (0, j))
-    return pl.pallas_call(
-        attend_kernel,
-        grid_spec=pltpu.PrefetchScalarGridSpec(
-            num_scalar_prefetch=1,
-            grid=(groups,),
-            in_specs=[own, full, full],
-            out_specs=[own, pl.BlockSpec((1, 8, rows), lambda j, p: (j, 0, 0))],
-        ),
-        out_shape=[
-            jax.ShapeDtypeStruct((rows, width), BF),
-            jax.ShapeDtypeStruct((groups, 8, rows), F32),
-        ],
-        compiler_params=limits(32),
-        cost_estimate=cost(16 * rows * slots * width, 5e6),
-        name="attend",
-    )(place, queries, keys, values)
-
-
-def attend_back(
-    place, queries, keys, values, grads, s, logs, cosine, sine, w_qkv, act_t, before, last, dp_size
-):
-    rows, width = queries.shape
-    slots = keys.shape[0]
-    groups = width // BLOCK
-    own = pl.BlockSpec((rows, BLOCK), lambda j, p: (0, j))
-    full = pl.BlockSpec((slots, BLOCK), lambda j, p: (0, j))
+    own = pl.BlockSpec((None, rows, BLOCK), lambda j, p: (at, 0, j))
+    full = pl.BlockSpec((None, slots, BLOCK), lambda j, p: (at, 0, j))
     own_table = pl.BlockSpec((rows, LANES), lambda j, p: (p[0], 0))
     full_table = pl.BlockSpec((slots, LANES), lambda j, p: (0, 0))
     every = pl.BlockSpec((1, width, 3 * BLOCK), lambda j, p: (j, 0, 0))
@@ -584,13 +590,15 @@
             in_specs=[
                 own, full, full,
                 pl.BlockSpec((None, rows, BLOCK), lambda j, p: (s, 0, j)),
-                pl.BlockSpec((1, 8, rows), lambda j, p: (j, 0, 0)),
+                pl.BlockSpec((None, 1, 8, rows), lambda j, p: (at, j, 0, 0)),
                 own_table, own_table, full_table, full_table,
                 pl.BlockSpec((width, BLOCK), lambda j, p: (0, j)),
                 pl.BlockSpec((width, BLOCK), lambda j, p: (0, groups + j)),
                 pl.BlockSpec((width, BLOCK), lambda j, p: (0, 2 * groups + j)),
-                whole(act_t),
-                pl.BlockSpec((width, rows), lambda j, p: (0, p[0])),
+                pl.BlockSpec(
+                    (None, width, slots), lambda j, p: (at, 0, 0), pipeline_mode=pl.Buffered(1)
+                ),
+                pl.BlockSpec((None, width, rows), lambda j, p: (at, 0, p[0])),
             ]
             + [every] * more,
             out_specs=[pl.BlockSpec((2, rows, width), lambda j, p: (0, 0, 0))] * 2 + weight_specs,
@@ -617,14 +625,15 @@
     )
 
 
-def norm_one_back(keep, core_got, near_got, tokens, grad_res, s, mod, gain, sums):
-    rows, width = tokens.shape
+def norm_one_back(keep, core_got, near_got, tokens, at, grad_res, s, mod, gain, sums):
+    _, rows, width = tokens.shape
     first = pl.BlockSpec((1, rows, width), lambda i: (0, 0, 0))
     return pl.pallas_call(
         functools.partial(norm_back_kernel, s, mod.shape[0]),
         grid=(1,),
         in_specs=[
-            first, first, whole(near_got), whole(tokens),
+            first, first, whole(near_got),
+            pl.BlockSpec((None, rows, width), lambda i: (at, 0, 0)),
             pl.BlockSpec((1, rows, width), lambda i: (s, 0, 0)),
             pl.BlockSpec((1,) + mod.shape[1:], lambda i: (s, 0, 0)),
             whole(gain), whole(sums),
@@ -636,18 +645,24 @@
             jax.ShapeDtypeStruct((rows, width), BF),
             jax.ShapeDtypeStruct(sums.shape, F32),
         ],
-        compiler_params=limits(),
+        compiler_params=limits(24),
         cost_estimate=cost(40 * rows * width, 6e6),
         name="norm_one_back",
     )(keep, core_got, near_got, tokens, grad_res, mod, gain, sums)
 
 
 def feed_forward(core, mixes, tokens, pulls, mod, gain, w_out, b_down, w_up, b_up, w_down, dp_size):
-    parts, rows, width = tokens.shape
+    parts, rows, width = pulls.shape
     hidden = w_up.shape[1]
     tile = width
     tiles = hidden // tile
     total = parts * rows
+    single = [
+        pl.BlockSpec(
+            (None, rows, width), lambda i, c, at=at: (at, 0, 0), pipeline_mode=pl.Buffered(1)
+        )
+        for _, at in mixes + tokens
+    ]
     blocks, piece = dp_size // 2, width // dp_size
     tall_piece = hidden // dp_size
     per_tile = tile // (2 * tall_piece)
@@ -660,9 +675,9 @@
     out_wide = pl.BlockSpec((blocks, piece, tile), lambda i, c: (0, 0, late(i)))
     out_tall = pl.BlockSpec((per_tile, tall_piece, width), lambda i, c: (last(i), 0, 0))
     outs = [
-        jax.ShapeDtypeStruct(tokens.shape, BF),
-        jax.ShapeDtypeStruct(tokens.shape, F32),
-        jax.ShapeDtypeStruct(tokens.shape, BF),
+        jax.ShapeDtypeStruct(pulls.shape, BF),
+        jax.ShapeDtypeStruct(pulls.shape, F32),
+        jax.ShapeDtypeStruct(pulls.shape, BF),
         jax.ShapeDtypeStruct((6 * parts + 2 + hidden // width + 8, width), F32),
         jax.ShapeDtypeStruct((blocks, piece, hidden + width), BF),
         jax.ShapeDtypeStruct((blocks, piece, hidden + width), BF),
@@ -674,8 +689,7 @@
         grid_spec=pltpu.PrefetchScalarGridSpec(
             num_scalar_prefetch=1,
             grid=(2 * tiles + 1,),
-            in_specs=[whole(m) for m in mixes]
-            + [whole(a) for a in (tokens, pulls, mod, gain, w_out, b_down)]
+            in_specs=single + [whole(a) for a in (pulls, mod, gain, w_out, b_down)]
             + [wide, bias, tall],
             out_specs=[whole(o) for o in outs[:4]]
             + [out_wide, out_wide, out_tall, out_tall],
@@ -696,7 +710,7 @@
         compiler_params=limits(),
         cost_estimate=cost(2 * total * width * (6 * hidden + 3 * width), 50e6),
         name="feed_forward",
-    )(core, *mixes, tokens, pulls, mod, gain, w_out, b_down, w_up, b_up, w_down)
+    )(core, *[v for v, _ in mixes + tokens], pulls, mod, gain, w_out, b_down, w_up, b_up, w_down)
 
 
 def combine(index, streams, turns, kept):
@@ -724,7 +738,7 @@
             num_scalar_prefetch=1, grid=(steps, turns), in_specs=in_specs, out_specs=out_specs
         ),
         out_shape=shapes,
-        compiler_params=limits(),
+        compiler_params=limits(60 if turns > 1 else 24),
         cost_estimate=cost(inputs[0].size * 4, inputs[0].size * 18),
         name="combine",
     )(index, *inputs)
@@ -747,7 +761,7 @@
             out_specs=[whole(v) for v in shapes],
         ),
         out_shape=shapes,
-        compiler_params=limits(),
+        compiler_params=limits(24),
         cost_estimate=cost(columns * rows * 8, columns * rows * 40),
         name="spread",
     )(place, *arrays)
@@ -760,7 +774,7 @@
         in_specs=[pl.BlockSpec((1,) + far.shape, lambda i: (0, 0, 0))] * 2 + [whole(far)],
         out_specs=[whole(v) for v in shapes],
         out_shape=shapes,
-        compiler_params=limits(),
+        compiler_params=limits(24),
         cost_estimate=cost(far.size * 2, far.size * 12),
         name="place_weights",
     )(own, near, far)
@@ -811,12 +825,11 @@
     def regroup(value, moving=None):
         return settle(value, send_across(value if moving is None else moving))
 
-    *sorted_tokens, both, order = arrange(lengths, tokens, cond.astype(F32))
+    first_tokens, rest_tokens, both, order = arrange(lengths, tokens, cond.astype(F32))
 
     puts = jnp.concatenate([order[:parts], stays.astype(jnp.int32)[None]])
 
-    mine = [None] * parts
-    mine[0] = regroup(sorted_tokens[0])
+    mine_first = regroup(first_tokens)
     both = jnp.where(stays, both, dp_swap(both, 0))
     cond_here, lengths_here = both[:parts, :-LANES].astype(BF), both[:, -1].astype(jnp.int32)
     mod = jnp.dot(cond_here, w_ada, preferred_element_type=F32) + b_ada
@@ -831,48 +844,37 @@
     sine = jnp.asarray(np.tile(np.concatenate([-sine, sine], 1), (1, LANES // HD)).astype(np.float32))
     gain_one_row, gain_two_row = gain_one[None, :], gain_two[None, :]
 
-    saved, mixes = [], []
     tie = lax.optimization_barrier
     forth = list(range(1, dp_bits))
     back = forth[::-1]
     halves = [jnp.stack([bit_of("dp", i), bit_of("dp", j)]) for i, j in zip(forth, back)]
     own_seq = seq[None]
-    mine[0] = after(mine[0], mod, *places, *halves, own_seq, puts, core_index)
-    nears = [seq_swap(mine[0], 0)]
-    moving = send_across(after(sorted_tokens[1], mine[0]))
-    fars = [dp_swap(mine[0], 0)]
-    mine[1] = settle(sorted_tokens[1], moving)
-    nears.append(seq_swap(mine[1], 0))
-    if parts > 2:
-        moving = send_across(after(sorted_tokens[2], mine[1]))
-    pulls, pulled = arrange_pulls(order, after(cotangent, mine[0])), []
-    for s in range(parts):
-        group = (mine[s], nears[s], fars[s], dp_swap(nears[s], 0))
-        group = tie((group, mixes[-1] if s else mine[1], tuple(pulled) if s > 1 else ()))[0]
-        if s == parts - 1:
-            pulled += [send_across(after(pulls[k], nears[s])) for k in range(len(pulled), parts)]
-        act_t, queries, keys, values = prepare(
-            places[s], group, mod, s, gain_one_row, w_qkv, cosine, sine
-        )
-        if s == parts - 1:
-            queries = after(queries, *pulled)
-        mixture, logs = attend(places[s], queries, keys, values)
-        saved.append((act_t, queries, keys, values, logs))
-        mixes.append(mixture)
-        if s + 1 < parts:
-            nears[s + 1] = after(nears[s + 1], mixture)
-            fars.append(dp_swap(after(mine[s + 1], mixture), 0))
-        if s + 2 < parts:
-            mine[s + 2] = settle(sorted_tokens[s + 2], moving, mixture)
-            nears.append(seq_swap(mine[s + 2], 0))
-            if s == 0:
-                pulled += [send_across(after(pulls[k], mine[2])) for k in range(parts - 1)]
-            if s + 3 < parts:
-                moving = send_across(after(sorted_tokens[s + 3], mine[s + 2]))
-    pulls = [settle(v, m, mixes[-1]) for v, m in zip(pulls, pulled)]
+    first_place = jnp.concatenate([own[None], lengths_here[:1]])
+    rest_place = jnp.concatenate([own[None], lengths_here[1:]])
+    mine_first = after(
+        mine_first, mod, *places, *halves, own_seq, puts, core_index, first_place, rest_place
+    )
+    near = seq_swap(mine_first, 0)
+    moving = send_across(rest_tokens)
+    far = dp_swap(mine_first, 0)
+    mine_rest = settle(rest_tokens, moving)
+    group = (mine_first, near, far, dp_swap(near, 0))
+    mine_rest = after(mine_rest, *group)
+    near_rest, far_rest = seq_swap(mine_rest, 0), dp_swap(mine_rest, 0)
+    pulls = arrange_pulls(order, after(cotangent, mine_first))
+    group = tie((group, mine_rest))[0]
+    fronts = [front(first_place, group, mod, 0, gain_one_row, w_qkv, cosine, sine)]
+    near_rest, far_rest, pulls, _ = tie((near_rest, far_rest, pulls, fronts[0][4]))
+    pulled = send_across(after(pulls, near_rest))
+    group = (mine_rest, near_rest, far_rest, dp_swap(near_rest, 0))
+    fronts.append(front(rest_place, group, mod, 1, gain_one_row, w_qkv, cosine, sine))
+    pulls = settle(pulls, pulled, fronts[1][4])
+    where = [(0, 0)] + [(1, k) for k in range(parts - 1)]
+    mine = [((mine_first, mine_rest)[f], at) for f, at in where]
+    mixes = [(fronts[f][4], at) for f, at in where]
 
     output, grad_res, grad_mix, sums, keep_up, send_up, keep_down, send_down = feed_forward(
-        core_index, mixes, jnp.stack(mine), jnp.stack(pulls), mod, gain_two_row, w_out,
+        core_index, mixes, mine, pulls, mod, gain_two_row, w_out,
         b_down[None, :], w_up, b_up[None, :], w_down, dp_size,
     )
     output_moved = send_across(output)
@@ -929,7 +931,7 @@
 
     def finish(s, sums):
         grad, rounded, sums = norm_one_back(
-            shares[s][0], cores[s], nears[s], mine[s], grad_res, s, mod, gain_one_row, sums
+            shares[s][0], cores[s], nears[s], *mine[s], grad_res, s, mod, gain_one_row, sums
         )
         grad_tokens.append(grad)
         return rounded, sums
@@ -939,9 +941,10 @@
 
     waits, weights = [], [None]
     for s in range(parts):
-        act_t, queries, keys, values, logs = saved[s]
+        at = where[s][1]
+        act_t, queries, keys, values, _, logs = fronts[where[s][0]]
         keep, send, *weights = attend_back(
-            places[s], after(queries, *waits), keys, values, grad_mix, s, logs, cosine,
+            places[s], at, after(queries, *waits), keys, values, grad_mix, s, logs, cosine,
             sine, w_qkv, act_t, weights[0], s == parts - 1, dp_size,
         )
         if s == 0:
@@ -965,78 +968,77 @@
             rounded, sums = finish(s - 1, sums)
             give_back(s - 1, rounded)
             waits.append(rounded)
+        cores[-1] = after(cores[-1], *waits)
         waits.append(pass_on(s))
 
     while mlp.orders[0]:
         mlp.merge()
         mlp.move()
+    waits = mlp.spread(True)
+    mlp.send()
     att = Halving([weights[0], weights[2]], [weights[1], weights[3]], 1)
+    cores[-1] = after(cores[-1], *waits)
+    passed = pass_on(parts - 1)
+    nears[-2] = after(nears[-2], passed)
     rounded, sums = finish(parts - 2, sums)
-    cores[-1] = after(cores[-1], rounded)
-    passed = pass_on(parts - 1)
-    give_back(parts - 2, after(rounded, passed))
-    att.got = tie((att.got, passed))[0]
+    give_back(parts - 2, rounded)
+    att.got = tie((att.got, rounded))[0]
     waits = att.merge()
     att.move()
-    mlp.got = tie((mlp.got, *waits))[0]
-    waits = mlp.spread(True)
-    nears[-1], mlp.sends = tie((nears[-1], mlp.sends, *waits))[:2]
-    mlp.send()
-    rounded, sums = finish(parts - 1, sums)
-    across = dp_swap(sums, 0)
-    give_back(parts - 1, rounded)
-    waits = [rounded]
     while att.orders[0]:
         att.got = tie((att.got, *waits))[0]
         waits = att.merge()
         att.move()
-    held = sums + after(across, *waits)
-    across = seq_swap(held, 0)
-    mlp.got, moved[-2] = tie((mlp.got, moved[-2], held))[:2]
+    mlp.got, mlp.own = tie((mlp.got, mlp.own, *waits))[:2]
     further = (mlp.own[1] + mlp.got[0][1].astype(F32)).astype(BF)
     att.got = tie((att.got, further))[0]
+    further = seq_swap(further, 1)
     waits = att.spread(True)
-    held = held + after(across, *waits)
     att.send()
-    further = seq_swap(further, 1)
+    nears[-1] = after(nears[-1], *waits)
+    rounded, sums = finish(parts - 1, sums)
+    give_back(parts - 1, rounded)
+    held = sums + dp_swap(sums, 0)
+    across = seq_swap(held, 0)
+    att.got, att.own, moved[-2] = tie((att.got, att.own, moved[-2], held))[:3]
+    later = (att.own[1] + att.got[0][1].astype(F32)).astype(BF)
+    held = held + after(across, later)
+    later = seq_swap(later, 1)
+
     count, kept = 6 * parts, held.shape[0] - 7
     conds = cond_here.astype(F32).reshape(1, -1)
     conds = jnp.pad(conds, ((0, 0), (0, width - conds.shape[1])))
     ours = jnp.concatenate([held[:kept], conds]).astype(BF)[None]
     got = swap(ours, "seq", 1)
-    mod_here = jnp.where(stays, held[:count], got[0, :count].astype(F32))
-    ours = jnp.concatenate([ours, got])
-    for bit in forth:
-        got = swap(ours, "dp", bit)
-        if bit == forth[0]:
-            att.got = tie((att.got, ours))[0]
-            later = (att.own[1] + att.got[0][1].astype(F32)).astype(BF)
-            got = after(got, later)
-            later = seq_swap(later, 1)
-        ours = jnp.concatenate([ours, got])
-    ours = ours.astype(F32)
-    totals = jnp.sum(ours[:, count:kept], axis=0)
-    output, g_tokens = put(puts, output, output_moved, grad_tokens, tie((tuple(moved), ours))[0])
-    piece = width // (dp_size * seq_size)
-    tall = hidden // (dp_size * seq_size)
+    piece, tall = width // (dp_size * seq_size), hidden // (dp_size * seq_size)
     shapes = [
         jax.ShapeDtypeStruct((piece, hidden), F32),
         jax.ShapeDtypeStruct((piece, width), F32),
         jax.ShapeDtypeStruct((tall, width), F32),
     ]
     g_w_up, g_w_out, g_w_down = place_weights(
-        place_mlp_kernel, mlp.own, mlp.got[0], after(further, g_tokens), shapes
+        place_mlp_kernel, mlp.own, mlp.got[0], after(further, ours), shapes
     )
-    shapes = [jax.ShapeDtypeStruct((piece, 3 * width), F32)]
-    (g_w_qkv,) = place_weights(
-        place_att_kernel, att.own, att.got[0], after(later, g_w_out), shapes
-    )
-
-    w_ada_f = w_ada.astype(F32)
+    got = after(got, g_w_up)
+    mod_here = jnp.where(stays, held[:count], got[0, :count].astype(F32))
+    ours = jnp.concatenate([ours, got])
+    for bit in forth:
+        got = swap(ours, "dp", bit)
+        if bit == forth[-1]:
+            shapes = [jax.ShapeDtypeStruct((piece, 3 * width), F32)]
+            (g_w_qkv,) = place_weights(
+                place_att_kernel, att.own, att.got[0], after(later, ours), shapes
+            )
+            moved[-1] = after(moved[-1], g_w_qkv)
+            output, g_tokens = put(puts, output, output_moved, grad_tokens, tuple(moved))
+            got = after(got, g_tokens)
+        ours = jnp.concatenate([ours, got])
+    ours = ours.astype(F32)
+    totals = jnp.sum(ours[:, count:kept], axis=0)
     g_cond = sum(
         jnp.dot(
             mod_here[k * parts : (k + 1) * parts],
-            w_ada_f[:, k * width : (k + 1) * width].T,
+            w_ada[:, k * width : (k + 1) * width].astype(F32).T,
             precision=HIGH,
         )
         for k in range(6)

time: 348 us -> 335 us (0.963)
  Pallas kernels: 173 us -> 147 us
  waiting for transfers between devices: 32.5 us -> 47.2 us
  local copies, waits for them, and re-layouts: 25.1 us -> 33.6 us
  starting transfers between devices: 91.3 us -> 87.8 us
    ppermute x10 -> x9, waiting for transfers between devices: 7.72 us -> 19.6 us  [seq_swap(): lax.ppermute(value, 'seq', [(i, i ^ 1 << bit) for i in range(seq_size)])]
    unnamed x144 -> x138, local copies, waits for them, and re-layouts: 18.9 us -> 27.3 us
    pallas_call x4, Pallas kernels: 21.8 us -> 13.7 us  [combine(): pl.pallas_call(combine_kernel, grid_spec=pltpu.PrefetchScalarGridSpec(num...]
    pallas_call x3, Pallas kernels: 11 us -> 4.41 us  [norm_one_back(): pl.pallas_call(functools.partial(norm_back_kernel, s, mod.shape[0]), grid...]
    pallas_call x2, Pallas kernels: 5.86 us -> 0.37 us  [spread(): pl.pallas_call(spread_kernel, grid_spec=pltpu.PrefetchScalarGridSpec(num_...]
    ppermute x25 -> x23, starting transfers between devices: 62.6 us -> 59.3 us  [dp_swap(): lax.ppermute(value, 'dp', [(i, i ^ 1 << bit) for i in range(dp_size)])]
    ppermute x25 -> x23, waiting for transfers between devices: 24.7 us -> 27.6 us  [dp_swap(): lax.ppermute(value, 'dp', [(i, i ^ 1 << bit) for i in range(dp_size)])]
    ppermute x10 -> x7, starting transfers between devices: 9.72 us -> 7.12 us  [send_across(): return lax.ppermute(value, ('dp', 'seq'), pairs)]
  transfers between devices with their start and end apart: 47 -> 41, of which waited for: 11 -> 15; matrix products, arithmetic and copies ran while one was open for 6% -> 5% of each run, Pallas kernels for 33% -> 29%
where the time goes in v1:
time: 335 us; the launch traced here: 333 us
  Pallas kernels  147 us (44%)
  starting transfers between devices  87.8 us (26%)
  waiting for transfers between devices  47.2 us (14%)
  local copies, waits for them, and re-layouts  33.6 us (10%)
  other arithmetic  11.9 us (4%)
  matrix products  4.08 us (1%)
    ppermute x23, starting transfers between devices, dp_swap(): lax.ppermute(value, 'dp', [(i, i ^ 1 << bit) for i in range(dp_size)])  59.3 us
    pallas_call x3, Pallas kernels, attend_back(): pl.pallas_call(functools.partial(attend_back_kernel, more, last), grid_sp...  49 us
    pallas_call x1, Pallas kernels, feed_forward(): pl.pallas_call(mlp_kernel, grid_spec=pltpu.PrefetchScalarGridSpec(num_sca...  41.9 us
    pallas_call x2, Pallas kernels, front(): pl.pallas_call(front_kernel, grid_spec=pltpu.PrefetchScalarGridSpec(num_s...  28 us
    ppermute x23, waiting for transfers between devices, dp_swap(): lax.ppermute(value, 'dp', [(i, i ^ 1 << bit) for i in range(dp_size)])  27.6 us
    unnamed x138, local copies, waits for them, and re-layouts  27.3 us
    ppermute x9, waiting for transfers between devices, seq_swap(): lax.ppermute(value, 'seq', [(i, i ^ 1 << bit) for i in range(seq_size)])  19.6 us
    ppermute x9, starting transfers between devices, seq_swap(): lax.ppermute(value, 'seq', [(i, i ^ 1 << bit) for i in range(seq_size)])  17.7 us
  transfers between devices with their start and end apart: 41, of which 15 were waited for; matrix products, arithmetic and copies ran while one was open for 5% of the time, Pallas kernels for 29%

profile of v1, /device:TPU:0, one launch (start us, length us, event | category | flops | bytes accessed | tf_op | source)
XLA Modules:
  0.0 332.8 jit_solution(17638018714652878163)
XLA Ops:
  9.1 1.9 add_add_fusion
  15.5 2.7 collective-permute-start.2
  18.2 10.8 %collective-permute-start.3 = (bf16[1,256,768]{2,1,0:T(8,128)(2,1)S(1)}, bf16[1,256,768]{2,1,0:T(8,128)(2,1)S(1)}, u32[]{:S(2)}, u32[]{:S(2)}) collective-permute-start(bf16[1,256,768]{2,1,0:T(8,128)(2,1)S(1)} %broadcast_select_fusion.2.a_ref.tok0_ref.tok_ref), channel_id=1, source_target_pairs={{0,4},{4,0},{8,12},{12,8},{16,20},{20,16},{24,28},{28,24},{1,5},{5... | collective-permute-start | bytes 1179656 | tf_op jit(solution)/shard_map/ppermute | solution.py:802
  29.0 12.2 %collective-permute-start.4 = (bf16[1,256,768]{2,1,0:T(8,128)(2,1)S(1)}, bf16[1,256,768]{2,1,0:T(8,128)(2,1)S(1)}, u32[]{:S(2)}, u32[]{:S(2)}) collective-permute-start(bf16[1,256,768]{2,1,0:T(8,128)(2,1)S(1)} %collective-permute-done.2.b_ref), channel_id=1, source_target_pairs={{0,4},{4,0},{8,12},{12,8},{16,20},{20,16},{24,28},{28,24},{1,5},{5... | collective-permute-start | bytes 1179656 | tf_op jit(solution)/shard_map/ppermute | solution.py:802
  43.7 8.8 %front.2 = (bf16[1,768,1024]{2,1,0:T(8,128)(2,1)S(1)}, bf16[1,256,768]{2,1,0:T(8,128)(2,1)S(1)}, bf16[1,1024,768]{2,1,0:T(8,128)(2,1)S(1)}, bf16[1,1024,768]{2,1...) custom-call(s32[2]{0:T(128)S(1)} %get-tuple-element.271.place, ...), custom_call_target="tpu_custom_call" | custom-call | flops 3623878 | bytes 15000 | tf_op jit(solution)/shard_map/front/pallas_call | solution.py:530
  58.1 4.2 %collective-permute-done.6.b_ref = bf16[2,256,768]{2,1,0:T(8,128)(2,1)S(1)} collective-permute-done((bf16[2,256,768]{2,1,0:T(8,128)(2,1)S(1)}, bf16[2,256,768]{2,1,0:T(8,128)(2,1)S(1)}, u32[]{:S(2)}, u32[]{:S(2)}) %collective-permute-start.6) | collective-permute-done | bytes 786464 | tf_op jit(solution)/shard_map/ppermute | solution.py:805
  63.2 3.9 %collective-permute-start.8 = (bf16[2,256,768]{2,1,0:T(8,128)(2,1)S(1)}, bf16[2,256,768]{2,1,0:T(8,128)(2,1)S(1)}, u32[]{:S(2)}, u32[]{:S(2)}) collective-permute-start(bf16[2,256,768]{2,1,0:T(8,128)(2,1)S(1)} %collective-permute-done.6.b_ref), channel_id=1, source_target_pairs={{0,4},{4,0},{8,12},{12,8},{16,20},{20,16},{24,28},{28,24},{1,5},{5... | collective-permute-start | bytes 2359304 | tf_op jit(solution)/shard_map/ppermute | solution.py:802
  69.0 19.2 %front.3 = (bf16[2,768,1024]{2,1,0:T(8,128)(2,1)S(1)}, bf16[2,256,768]{2,1,0:T(8,128)(2,1)S(1)}, bf16[2,1024,768]{2,1,0:T(8,128)(2,1)S(1)}, bf16[2,1024,768]{2,1...) custom-call(s32[8]{0:T(128)S(1)} %pad_add_fusion.4.place, ...), custom_call_target="tpu_custom_call" | custom-call | flops 7247757 | bytes 30000 | tf_op jit(solution)/shard_map/front/pallas_call | solution.py:530
  93.7 41.9 %feed_forward.1 = (bf16[3,256,768]{2,1,0:T(8,128)(2,1)}, f32[3,256,768]{2,1,0:T(8,128)}, bf16[3,256,768]{2,1,0:T(8,128)(2,1)}, f32[32,768]{1,0:T(8,128)}, bf16[4...) custom-call(s32[1]{0:T(128)} %bitcast.1.core, ...), custom_call_target="tpu_custom_call" | custom-call | flops 24461180 | bytes 50000 | tf_op jit(solution)/shard_map/feed_forward/pallas_call | solution.py:687
  136.6 15.8 %attend_back.3 = (f32[2,256,768]{2,1,0:T(8,128)}, bf16[2,256,768]{2,1,0:T(8,128)(2,1)}, f32[3,768,768]{2,1,0:T(8,128)}) custom-call(s32[3]{0:T(128)} %get-tuple-element.273.place, bf16[1,256,768]{2,1,0:T(8,128)(2,1)} %copy-done.49, bf16[1,1024,768]{2,1,0:T(8,128)(2,1)} %copy-done.32, bf16[1,1024,768]{2,1,0:T(8,128)(2,1)} %copy-done.33, ...), custom_call_target="tpu_custom_call" | custom-call | flops 12079595 | bytes 12000 | tf_op jit(solution)/shard_map/attend_back/pallas_call | solution.py:585
  154.0 8.5 %combine.4 = (bf16[2,96,3840]{2,1,0:T(8,128)(2,1)}, bf16[2,96,3840]{2,1,0:T(8,128)(2,1)}, bf16[2,384,768]{2,1,0:T(8,128)(2,1)}, bf16[2,384,768]{2,1,0:T(8,128)(2,1)}) custom-call(s32[2]{0:T(128)} %get-tuple-element.272.index, bf16[2,2,1,96,3840]{4,3,2,1,0:T(8,128)(2,1)} %bitcast.110, bf16[2,2,1,96,3840]{4,3,2,1,0:T(8,128)(2,1)} %bitcast.112, ...), custom_call_target="tpu_custom_call" | custom-call | flops 5898 | bytes 26542 | tf_op jit(solution)/shard_map/combine/pallas_call | solution.py:735
  162.5 13.3 %collective-permute-start.13 = (bf16[2,96,3840]{2,1,0:T(8,128)(2,1)}, bf16[2,96,3840]{2,1,0:T(8,128)(2,1)S(1)}, u32[]{:S(2)}, u32[]{:S(2)}) collective-permute-start(bf16[2,96,3840]{2,1,0:T(8,128)(2,1)} %get-tuple-element.172), channel_id=1, source_target_pairs={{0,8},{4,12},{8,0},{12,4},{16,24},{20,28},{24,16},{28,20},{1,9},{5... | collective-permute-start | bytes 4423688 | tf_op jit(solution)/shard_map/ppermute | solution.py:802
  179.1 17.7 %attend_back.4 = (f32[2,256,768]{2,1,0:T(8,128)}, bf16[2,256,768]{2,1,0:T(8,128)(2,1)}, f32[3,768,768]{2,1,0:T(8,128)}) custom-call(s32[3]{0:T(128)} %get-tuple-element.274.place, bf16[2,256,768]{2,1,0:T(8,128)(2,1)} %copy-done.24, bf16[2,1024,768]{2,1,0:T(8,128)(2,1)} %copy-done.7, bf16[2,1024,768]{2,1,0:T(8,128)(2,1)} %get-tuple-element.179.v_ref, ...), custom_call_target="tpu_custom_call" | custom-call | flops 12079595 | bytes 12000 | tf_op jit(solution)/shard_map/attend_back/pallas_call | solution.py:585
  196.9 6.3 %collective-permute-done.14 = bf16[2,384,768]{2,1,0:T(8,128)(2,1)} collective-permute-done((bf16[2,384,768]{2,1,0:T(8,128)(2,1)}, bf16[2,384,768]{2,1,0:T(8,128)(2,1)}, u32[]{:S(2)}, u32[]{:S(2)}) %collective-permute-start.14) | collective-permute-done | bytes 1179680 | tf_op jit(solution)/shard_map/ppermute | solution.py:802
  203.9 4.7 %collective-permute-done.13 = bf16[2,96,3840]{2,1,0:T(8,128)(2,1)S(1)} collective-permute-done((bf16[2,96,3840]{2,1,0:T(8,128)(2,1)}, bf16[2,96,3840]{2,1,0:T(8,128)(2,1)S(1)}, u32[]{:S(2)}, u32[]{:S(2)}) %collective-permute-start.13) | collective-permute-done | bytes 1474592 | tf_op jit(solution)/shard_map/ppermute | solution.py:802
  212.5 3.6 %combine.5 = (f32[1,96,3840]{2,1,0:T(8,128)S(1)}, bf16[1,96,3840]{2,1,0:T(8,128)(2,1)}, f32[1,384,768]{2,1,0:T(8,128)S(1)}, bf16[1,384,768]{2,1,0:T(8,128)(2,1)}) custom-call(s32[2]{0:T(128)S(1)} %pad_add_fusion.3.index, bf16[1,2,1,96,3840]{4,3,2,1,0:T(8,128)(2,1)S(1)} %bitcast.82, bf16[1,2,1,96,3840]{4,3,2,1,0:T(8,128)(2,1)S(1)} %bitcast.84, ...), custom_call_target="tpu_custom_call" | custom-call | flops 2949 | bytes 13271 | tf_op jit(solution)/shard_map/combine/pallas_call | solution.py:735
  218.3 2.1 collective-permute-start.18
  220.4 1.8 collective-permute-start.19
  226.3 15.5 %attend_back.5 = (f32[2,256,768]{2,1,0:T(8,128)}, bf16[2,256,768]{2,1,0:T(8,128)(2,1)}, f32[4,96,1152]{2,1,0:T(8,128)}, bf16[4,96,1152]{2,1,0:T(8,128)(2,1)}, f3...) custom-call(s32[3]{0:T(128)} %add_add_fusion.2.place, bf16[2,256,768]{2,1,0:T(8,128)(2,1)} %copy-done.24, ...), custom_call_target="tpu_custom_call" | custom-call | flops 12079595 | bytes 12000 | tf_op jit(solution)/shard_map/attend_back/pallas_call | solution.py:585
  241.8 3.2 collective-permute-start.22
  251.0 2.0 norm_one_back.4
  256.7 2.7 collective-permute-start.27
  262.0 5.0 %collective-permute-done.26 = bf16[2,96,1152]{2,1,0:T(8,128)(2,1)S(1)} collective-permute-done((bf16[2,96,1152]{2,1,0:T(8,128)(2,1)S(1)}, bf16[2,96,1152]{2,1,0:T(8,128)(2,1)S(1)}, u32[]{:S(2)}, u32[]{:S(2)}) %collective-permute-start.26) | collective-permute-done | bytes 442400 | tf_op jit(solution)/shard_map/ppermute | solution.py:802
  267.1 2.4 collective-permute-done.27
  273.3 3.6 %collective-permute-done.28 = bf16[1,96,1152]{2,1,0:T(8,128)(2,1)S(1)} collective-permute-done((bf16[1,96,1152]{2,1,0:T(8,128)(2,1)S(1)}, bf16[1,96,1152]{2,1,0:T(8,128)(2,1)S(1)}, u32[]{:S(2)}, u32[]{:S(2)}) %collective-permute-start.28) | collective-permute-done | bytes 221216 | tf_op jit(solution)/shard_map/ppermute | solution.py:802
  282.4 6.7 %collective-permute-start.38 = (bf16[24,6912]{1,0:T(8,128)(2,1)}, bf16[24,6912]{1,0:T(8,128)(2,1)S(1)}, u32[]{:S(2)}, u32[]{:S(2)}) collective-permute-start(bf16[24,6912]{1,0:T(8,128)(2,1)} %fusion.3), channel_id=1, source_target_pairs={{0,2},{1,3},{2,0},{3,1},{4,6},{5,7},{6,4},{7,5},{8,10},{9,11},{10,... | collective-permute-start | bytes 995336 | tf_op jit(solution)/shard_map/ppermute | solution.py:805
  290.4 8.7 %collective-permute-done.36 = f32[32,768]{1,0:T(8,128)S(1)} collective-permute-done((f32[32,768]{1,0:T(8,128)S(1)}, f32[32,768]{1,0:T(8,128)S(1)}, u32[]{:S(2)}, u32[]{:S(2)}) %collective-permute-start.36) | collective-permute-done | bytes 98336 | tf_op jit(solution)/shard_map/ppermute | solution.py:805
  299.2 2.0 collective-permute-start.37
  302.0 3.4 %collective-permute-start.35 = (bf16[24,2304]{1,0:T(8,128)(2,1)S(1)}, bf16[24,2304]{1,0:T(8,128)(2,1)S(1)}, u32[]{:S(2)}, u32[]{:S(2)}) collective-permute-start(bf16[24,2304]{1,0:T(8,128)(2,1)S(1)} %fusion.11), channel_id=1, source_target_pairs={{0,2},{1,3},{2,0},{3,1},{4,6},{5,7},{6,4},{7,5},{8,10},{9,11},{10,... | collective-permute-start | bytes 331784 | tf_op jit(solution)/shard_map/ppermute | solution.py:805
  309.7 1.9 collective-permute-done.39
  314.2 6.1 %collective-permute-done.35.far_ref = bf16[24,2304]{1,0:T(8,128)(2,1)S(1)} collective-permute-done((bf16[24,2304]{1,0:T(8,128)(2,1)S(1)}, bf16[24,2304]{1,0:T(8,128)(2,1)S(1)}, u32[]{:S(2)}, u32[]{:S(2)}) %collective-permute-start.35) | collective-permute-done | bytes 110624 | tf_op jit(solution)/shard_map/ppermute | solution.py:805
  321.8 5.9 %put.1 = (bf16[3,256,768]{2,1,0:T(8,128)(2,1)}, f32[3,256,768]{2,1,0:T(8,128)}) custom-call(s32[4]{0:T(128)} %pad_add_fusion.order, bf16[3,256,768]{2,1,0:T(8,128)(2,1)} %get-tuple-element.156.refs_0_, bf16[3,256,768]{2,1,0:T(8,128)(2,1)} %collective-permute-done.16.refs_1_, f32[256,768]{1,0:T(8,128)} %copy-done.44, f32[256,768]{1,0:T(8,128)} %copy-done.45, ...), custom_call_target="tpu_custom_call" | custom-call | flops 1000 | bytes 10000 | tf_op jit(solution)/shard_map/put/pallas_call | solution.py:505
  (267 shorter events, 82.9 us)
Async XLA Ops:
  4.9 10.5 %collective-permute-start.1 = (bf16[1,256,768]{2,1,0:T(8,128)(2,1)S(1)}, bf16[1,256,768]{2,1,0:T(8,128)(2,1)S(1)}, u32[]{:S(2)}, u32[]{:S(2)}) collective-permute-start(bf16[1,256,768]{2,1,0:T(8,128)(2,1)S(1)} %get-tuple-element.140), channel_id=1, source_target_pairs={{2,4},{3,5},{4,2},{5,3},{10,12},{11,13},{12,10},{13,11},{18,20},{1... | collective-permute-start | bytes 1179656 | tf_op jit(solution)/shard_map/ppermute | solution.py:820
  5.6 35.5 %collective-permute-start.5 = (bf16[2,256,768]{2,1,0:T(8,128)(2,1)S(1)}, bf16[2,256,768]{2,1,0:T(8,128)(2,1)S(1)}, u32[]{:S(2)}, u32[]{:S(2)}) collective-permute-start(bf16[2,256,768]{2,1,0:T(8,128)(2,1)S(1)} %get-tuple-element.142), channel_id=1, source_target_pairs={{2,4},{3,5},{4,2},{5,3},{10,12},{11,13},{12,10},{13,11},{18,20},{1... | collective-permute-start | bytes 2359304 | tf_op jit(solution)/shard_map/ppermute | solution.py:820
  15.5 13.4 %collective-permute-start.2 = (bf16[1,256,768]{2,1,0:T(8,128)(2,1)S(1)}, bf16[1,256,768]{2,1,0:T(8,128)(2,1)S(1)}, u32[]{:S(2)}, u32[]{:S(2)}) collective-permute-start(bf16[1,256,768]{2,1,0:T(8,128)(2,1)S(1)} %broadcast_select_fusion.2.a_ref.tok0_ref.tok_ref), channel_id=1, source_target_pairs={{0,1},{1,0},{2,3},{3,2},{4,5},{5,4},{6,7},{7,6},{8,9},{9,8},{10,11... | collective-permute-start | bytes 1179656 | tf_op jit(solution)/shard_map/ppermute | solution.py:805
  18.2 23.1 %collective-permute-start.3 = (bf16[1,256,768]{2,1,0:T(8,128)(2,1)S(1)}, bf16[1,256,768]{2,1,0:T(8,128)(2,1)S(1)}, u32[]{:S(2)}, u32[]{:S(2)}) collective-permute-start(bf16[1,256,768]{2,1,0:T(8,128)(2,1)S(1)} %broadcast_select_fusion.2.a_ref.tok0_ref.tok_ref), channel_id=1, source_target_pairs={{0,4},{4,0},{8,12},{12,8},{16,20},{20,16},{24,28},{28,24},{1,5},{5... | collective-permute-start | bytes 1179656 | tf_op jit(solution)/shard_map/ppermute | solution.py:802
  29.0 13.5 %collective-permute-start.4 = (bf16[1,256,768]{2,1,0:T(8,128)(2,1)S(1)}, bf16[1,256,768]{2,1,0:T(8,128)(2,1)S(1)}, u32[]{:S(2)}, u32[]{:S(2)}) collective-permute-start(bf16[1,256,768]{2,1,0:T(8,128)(2,1)S(1)} %collective-permute-done.2.b_ref), channel_id=1, source_target_pairs={{0,4},{4,0},{8,12},{12,8},{16,20},{20,16},{24,28},{28,24},{1,5},{5... | collective-permute-start | bytes 1179656 | tf_op jit(solution)/shard_map/ppermute | solution.py:802
  42.5 19.8 %collective-permute-start.6 = (bf16[2,256,768]{2,1,0:T(8,128)(2,1)S(1)}, bf16[2,256,768]{2,1,0:T(8,128)(2,1)S(1)}, u32[]{:S(2)}, u32[]{:S(2)}) collective-permute-start(bf16[2,256,768]{2,1,0:T(8,128)(2,1)S(1)} %broadcast_select_fusion.1.a_ref.tok1_ref.tok2_ref.tok_ref), channel_id=1, source_target_pairs={{0,1},{1,0},{2,3},{3,2},{4,5},{5,4},{6,7},{7,6},{8,9},{9,8},{10,11... | collective-permute-start | bytes 2359304 | tf_op jit(solution)/shard_map/ppermute | solution.py:805
  42.5 19.8 %collective-permute-start.7 = (bf16[2,256,768]{2,1,0:T(8,128)(2,1)S(1)}, bf16[2,256,768]{2,1,0:T(8,128)(2,1)S(1)}, u32[]{:S(2)}, u32[]{:S(2)}) collective-permute-start(bf16[2,256,768]{2,1,0:T(8,128)(2,1)S(1)} %broadcast_select_fusion.1.a_ref.tok1_ref.tok2_ref.tok_ref), channel_id=1, source_target_pairs={{0,4},{4,0},{8,12},{12,8},{16,20},{20,16},{24,28},{28,24},{1,5},{5... | collective-permute-start | bytes 2359304 | tf_op jit(solution)/shard_map/ppermute | solution.py:802
  62.3 29.3 %collective-permute-start.9 = (bf16[3,256,768]{2,1,0:T(8,128)(2,1)S(1)}, bf16[3,256,768]{2,1,0:T(8,128)(2,1)S(1)}, u32[]{:S(2)}, u32[]{:S(2)}) collective-permute-start(bf16[3,256,768]{2,1,0:T(8,128)(2,1)S(1)} %arrange_pulls.1), channel_id=1, source_target_pairs={{2,4},{3,5},{4,2},{5,3},{10,12},{11,13},{12,10},{13,11},{18,20},{1... | collective-permute-start | bytes 3538952 | tf_op jit(solution)/shard_map/ppermute | solution.py:820
  135.6 16.8 %collective-permute-start.10 = (bf16[4,96,3840]{2,1,0:T(8,128)(2,1)}, bf16[4,96,3840]{2,1,0:T(8,128)(2,1)S(1)}, u32[]{:S(2)}, u32[]{:S(2)}) collective-permute-start(bf16[4,96,3840]{2,1,0:T(8,128)(2,1)} %get-tuple-element.167), channel_id=1, source_target_pairs={{0,4},{4,0},{8,12},{12,8},{16,20},{20,16},{24,28},{28,24},{1,5},{5... | collective-permute-start | bytes 8847368 | tf_op jit(solution)/shard_map/ppermute | solution.py:802
  136.5 15.9 %collective-permute-start.11 = (bf16[4,384,768]{2,1,0:T(8,128)(2,1)}, bf16[4,384,768]{2,1,0:T(8,128)(2,1)}, u32[]{:S(2)}, u32[]{:S(2)}) collective-permute-start(bf16[4,384,768]{2,1,0:T(8,128)(2,1)} %get-tuple-element.168), channel_id=1, source_target_pairs={{0,4},{4,0},{8,12},{12,8},{16,20},{20,16},{24,28},{28,24},{1,5},{5... | collective-permute-start | bytes 7077896 | tf_op jit(solution)/shard_map/ppermute | solution.py:802
  162.5 46.1 %collective-permute-start.13 = (bf16[2,96,3840]{2,1,0:T(8,128)(2,1)}, bf16[2,96,3840]{2,1,0:T(8,128)(2,1)S(1)}, u32[]{:S(2)}, u32[]{:S(2)}) collective-permute-start(bf16[2,96,3840]{2,1,0:T(8,128)(2,1)} %get-tuple-element.172), channel_id=1, source_target_pairs={{0,8},{4,12},{8,0},{12,4},{16,24},{20,28},{24,16},{28,20},{1,9},{5... | collective-permute-start | bytes 4423688 | tf_op jit(solution)/shard_map/ppermute | solution.py:802
  175.8 21.1 %collective-permute-start.16 = (bf16[3,256,768]{2,1,0:T(8,128)(2,1)}, bf16[3,256,768]{2,1,0:T(8,128)(2,1)}, u32[]{:S(2)}, u32[]{:S(2)}) collective-permute-start(bf16[3,256,768]{2,1,0:T(8,128)(2,1)} %get-tuple-element.156.refs_0_), channel_id=1, source_target_pairs={{2,4},{3,5},{4,2},{5,3},{10,12},{11,13},{12,10},{13,11},{18,20},{1... | collective-permute-start | bytes 3538952 | tf_op jit(solution)/shard_map/ppermute | solution.py:820
  177.5 25.6 %collective-permute-start.14 = (bf16[2,384,768]{2,1,0:T(8,128)(2,1)}, bf16[2,384,768]{2,1,0:T(8,128)(2,1)}, u32[]{:S(2)}, u32[]{:S(2)}) collective-permute-start(bf16[2,384,768]{2,1,0:T(8,128)(2,1)} %get-tuple-element.173), channel_id=1, source_target_pairs={{0,16},{4,20},{8,24},{12,28},{16,0},{20,4},{24,8},{28,12},{1,17},{... | collective-permute-start | bytes 3538952 | tf_op jit(solution)/shard_map/ppermute | solution.py:802
  179.1 24.1 %collective-permute-start.15 = (bf16[256,768]{1,0:T(8,128)(2,1)}, bf16[256,768]{1,0:T(8,128)(2,1)S(1)}, u32[]{:S(2)}, u32[]{:S(2)}) collective-permute-start(bf16[256,768]{1,0:T(8,128)(2,1)} %fusion), channel_id=1, source_target_pairs={{0,1},{1,0},{2,3},{3,2},{4,5},{5,4},{6,7},{7,6},{8,9},{9,8},{10,11... | collective-permute-start | bytes 1179656 | tf_op jit(solution)/shard_map/ppermute | solution.py:805
  209.8 15.5 %collective-permute-start.17 = (bf16[2,256,768]{2,1,0:T(8,128)(2,1)}, bf16[2,256,768]{2,1,0:T(8,128)(2,1)S(1)}, u32[]{:S(2)}, u32[]{:S(2)}) collective-permute-start(bf16[2,256,768]{2,1,0:T(8,128)(2,1)} %get-tuple-element.191), channel_id=1, source_target_pairs={{0,4},{4,0},{8,12},{12,8},{16,20},{20,16},{24,28},{28,24},{1,5},{5... | collective-permute-start | bytes 2359304 | tf_op jit(solution)/shard_map/ppermute | solution.py:802
  218.3 23.5 %collective-permute-start.18 = (bf16[1,96,3840]{2,1,0:T(8,128)(2,1)}, bf16[1,96,3840]{2,1,0:T(8,128)(2,1)S(1)}, u32[]{:S(2)}, u32[]{:S(2)}) collective-permute-start(bf16[1,96,3840]{2,1,0:T(8,128)(2,1)} %get-tuple-element.196), channel_id=1, source_target_pairs={{0,16},{4,20},{8,24},{12,28},{16,0},{20,4},{24,8},{28,12},{1,17},{... | collective-permute-start | bytes 2211848 | tf_op jit(solution)/shard_map/ppermute | solution.py:802
  220.4 21.4 %collective-permute-start.19 = (bf16[1,384,768]{2,1,0:T(8,128)(2,1)}, bf16[1,384,768]{2,1,0:T(8,128)(2,1)S(1)}, u32[]{:S(2)}, u32[]{:S(2)}) collective-permute-start(bf16[1,384,768]{2,1,0:T(8,128)(2,1)} %get-tuple-element.197), channel_id=1, source_target_pairs={{0,8},{4,12},{8,0},{12,4},{16,24},{20,28},{24,16},{28,20},{1,9},{5... | collective-permute-start | bytes 1769480 | tf_op jit(solution)/shard_map/ppermute | solution.py:802
  223.8 17.9 %collective-permute-start.21 = (bf16[256,768]{1,0:T(8,128)(2,1)}, bf16[256,768]{1,0:T(8,128)(2,1)}, u32[]{:S(2)}, u32[]{:S(2)}) collective-permute-start(bf16[256,768]{1,0:T(8,128)(2,1)} %get-tuple-element.198), channel_id=1, source_target_pairs={{2,4},{3,5},{4,2},{5,3},{10,12},{11,13},{12,10},{13,11},{18,20},{1... | collective-permute-start | bytes 1179656 | tf_op jit(solution)/shard_map/ppermute | solution.py:820
  226.3 15.5 %collective-permute-start.20 = (bf16[256,768]{1,0:T(8,128)(2,1)}, bf16[256,768]{1,0:T(8,128)(2,1)}, u32[]{:S(2)}, u32[]{:S(2)}) collective-permute-start(bf16[256,768]{1,0:T(8,128)(2,1)} %fusion.1), channel_id=1, source_target_pairs={{0,1},{1,0},{2,3},{3,2},{4,5},{5,4},{6,7},{7,6},{8,9},{9,8},{10,11... | collective-permute-start | bytes 1179656 | tf_op jit(solution)/shard_map/ppermute | solution.py:805
  245.0 8.8 %collective-permute-start.24 = (bf16[4,96,1152]{2,1,0:T(8,128)(2,1)}, bf16[4,96,1152]{2,1,0:T(8,128)(2,1)S(1)}, u32[]{:S(2)}, u32[]{:S(2)}) collective-permute-start(bf16[4,96,1152]{2,1,0:T(8,128)(2,1)} %get-tuple-element.220), channel_id=1, source_target_pairs={{0,4},{4,0},{8,12},{12,8},{16,20},{20,16},{24,28},{28,24},{1,5},{5... | collective-permute-start | bytes 2654216 | tf_op jit(solution)/shard_map/ppermute | solution.py:802
  245.1 8.8 %collective-permute-start.25 = (bf16[4,96,1152]{2,1,0:T(8,128)(2,1)}, bf16[4,96,1152]{2,1,0:T(8,128)(2,1)S(1)}, u32[]{:S(2)}, u32[]{:S(2)}) collective-permute-start(bf16[4,96,1152]{2,1,0:T(8,128)(2,1)} %get-tuple-element.221), channel_id=1, source_target_pairs={{0,4},{4,0},{8,12},{12,8},{16,20},{20,16},{24,28},{28,24},{1,5},{5... | collective-permute-start | bytes 2654216 | tf_op jit(solution)/shard_map/ppermute | solution.py:802
  248.5 23.9 %collective-permute-start.30 = (bf16[2,24,6912]{2,1,0:T(8,128)(2,1)S(1)}, bf16[2,24,6912]{2,1,0:T(8,128)(2,1)S(1)}, u32[]{:S(2)}, u32[]{:S(2)}) collective-permute-start(bf16[2,24,6912]{2,1,0:T(8,128)(2,1)S(1)} %get-tuple-element.214), channel_id=1, source_target_pairs={{0,1},{1,0},{2,3},{3,2},{4,5},{5,4},{6,7},{7,6},{8,9},{9,8},{10,11... | collective-permute-start | bytes 1990664 | tf_op jit(solution)/shard_map/ppermute | solution.py:919
  254.8 12.2 %collective-permute-start.26 = (bf16[2,96,1152]{2,1,0:T(8,128)(2,1)S(1)}, bf16[2,96,1152]{2,1,0:T(8,128)(2,1)S(1)}, u32[]{:S(2)}, u32[]{:S(2)}) collective-permute-start(bf16[2,96,1152]{2,1,0:T(8,128)(2,1)S(1)} %get-tuple-element.227), channel_id=1, source_target_pairs={{0,8},{4,12},{8,0},{12,4},{16,24},{20,28},{24,16},{28,20},{1,9},{5... | collective-permute-start | bytes 1327112 | tf_op jit(solution)/shard_map/ppermute | solution.py:802
  256.7 12.8 %collective-permute-start.27 = (bf16[2,96,1152]{2,1,0:T(8,128)(2,1)S(1)}, bf16[2,96,1152]{2,1,0:T(8,128)(2,1)S(1)}, u32[]{:S(2)}, u32[]{:S(2)}) collective-permute-start(bf16[2,96,1152]{2,1,0:T(8,128)(2,1)S(1)} %get-tuple-element.228), channel_id=1, source_target_pairs={{0,16},{4,20},{8,24},{12,28},{16,0},{20,4},{24,8},{28,12},{1,17},{... | collective-permute-start | bytes 1327112 | tf_op jit(solution)/shard_map/ppermute | solution.py:802
  259.4 21.3 %collective-permute-start.23 = (bf16[256,768]{1,0:T(8,128)(2,1)S(1)}, bf16[256,768]{1,0:T(8,128)(2,1)S(1)}, u32[]{:S(2)}, u32[]{:S(2)}) collective-permute-start(bf16[256,768]{1,0:T(8,128)(2,1)S(1)} %fusion.2), channel_id=1, source_target_pairs={{0,1},{1,0},{2,3},{3,2},{4,5},{5,4},{6,7},{7,6},{8,9},{9,8},{10,11... | collective-permute-start | bytes 1179656 | tf_op jit(solution)/shard_map/ppermute | solution.py:805
  261.1 29.3 %collective-permute-start.32 = (bf16[256,768]{1,0:T(8,128)(2,1)S(1)}, bf16[256,768]{1,0:T(8,128)(2,1)S(1)}, u32[]{:S(2)}, u32[]{:S(2)}) collective-permute-start(bf16[256,768]{1,0:T(8,128)(2,1)S(1)} %get-tuple-element.222), channel_id=1, source_target_pairs={{2,4},{3,5},{4,2},{5,3},{10,12},{11,13},{12,10},{13,11},{18,20},{1... | collective-permute-start | bytes 1179656 | tf_op jit(solution)/shard_map/ppermute | solution.py:820
  278.1 12.3 %collective-permute-start.31 = (bf16[2,24,2304]{2,1,0:T(8,128)(2,1)S(1)}, bf16[2,24,2304]{2,1,0:T(8,128)(2,1)S(1)}, u32[]{:S(2)}, u32[]{:S(2)}) collective-permute-start(bf16[2,24,2304]{2,1,0:T(8,128)(2,1)S(1)} %get-tuple-element.241), channel_id=1, source_target_pairs={{0,1},{1,0},{2,3},{3,2},{4,5},{5,4},{6,7},{7,6},{8,9},{9,8},{10,11... | collective-permute-start | bytes 663560 | tf_op jit(solution)/shard_map/ppermute | solution.py:919
  282.4 23.2 %collective-permute-start.38 = (bf16[24,6912]{1,0:T(8,128)(2,1)}, bf16[24,6912]{1,0:T(8,128)(2,1)S(1)}, u32[]{:S(2)}, u32[]{:S(2)}) collective-permute-start(bf16[24,6912]{1,0:T(8,128)(2,1)} %fusion.3), channel_id=1, source_target_pairs={{0,2},{1,3},{2,0},{3,1},{4,6},{5,7},{6,4},{7,5},{8,10},{9,11},{10,... | collective-permute-start | bytes 995336 | tf_op jit(solution)/shard_map/ppermute | solution.py:805
  289.1 10.0 %collective-permute-start.36 = (f32[32,768]{1,0:T(8,128)S(1)}, f32[32,768]{1,0:T(8,128)S(1)}, u32[]{:S(2)}, u32[]{:S(2)}) collective-permute-start(f32[32,768]{1,0:T(8,128)S(1)} %add.60), channel_id=1, source_target_pairs={{0,1},{1,0},{2,3},{3,2},{4,5},{5,4},{6,7},{7,6},{8,9},{9,8},{10,11... | collective-permute-start | bytes 294920 | tf_op jit(solution)/shard_map/ppermute | solution.py:805
  301.2 19.8 %collective-permute-start.34 = (bf16[256,768]{1,0:T(8,128)(2,1)}, bf16[256,768]{1,0:T(8,128)(2,1)S(1)}, u32[]{:S(2)}, u32[]{:S(2)}) collective-permute-start(bf16[256,768]{1,0:T(8,128)(2,1)} %copy-done.56), channel_id=1, source_target_pairs={{2,4},{3,5},{4,2},{5,3},{10,12},{11,13},{12,10},{13,11},{18,20},{1... | collective-permute-start | bytes 1179656 | tf_op jit(solution)/shard_map/ppermute | solution.py:820
  302.0 18.2 %collective-permute-start.35 = (bf16[24,2304]{1,0:T(8,128)(2,1)S(1)}, bf16[24,2304]{1,0:T(8,128)(2,1)S(1)}, u32[]{:S(2)}, u32[]{:S(2)}) collective-permute-start(bf16[24,2304]{1,0:T(8,128)(2,1)S(1)} %fusion.11), channel_id=1, source_target_pairs={{0,2},{1,3},{2,0},{3,1},{4,6},{5,7},{6,4},{7,5},{8,10},{9,11},{10,... | collective-permute-start | bytes 331784 | tf_op jit(solution)/shard_map/ppermute | solution.py:805
  311.7 16.0 %collective-permute-start.40 = (bf16[4,26,768]{2,1,0:T(8,128)(2,1)S(1)}, bf16[4,26,768]{2,1,0:T(8,128)(2,1)S(1)}, u32[]{:S(2)}, u32[]{:S(2)}) collective-permute-start(bf16[4,26,768]{2,1,0:T(8,128)(2,1)S(1)} %pad_maximum_fusion.1), channel_id=1, source_target_pairs={{0,16},{4,20},{8,24},{12,28},{16,0},{20,4},{24,8},{28,12},{1,17},{... | collective-permute-start | bytes 479240 | tf_op jit(solution)/shard_map/ppermute | solution.py:802
  (76 other events, 561.0 us)
